TPU v7x, 32 devices: a whole 2x2x4 slice. The times are simulated.
32 devices in a mesh: rep: 2 (over x), fsdp: 4 (over y, core), tp: 4 (over z).
Axes of the slice: x: 2, y: 2, z: 4, core: 2. Of those that a mesh axis runs over, the one named last changes fastest.
Arguments:
- gate_up_master: float32 [2, 4096, 14336], P(None, 'fsdp', ('rep', 'tp')), may hold values from -0.09375 to 0.09375
- gate_up_moment: float32 [2, 4096, 14336], P(None, 'fsdp', ('rep', 'tp')), may hold values from -0.00018310547 to 0.00018310547
- gate_up_second: float32 [2, 4096, 14336], P(None, 'fsdp', ('rep', 'tp')), may hold values from 8.5149493e-10 to 8.51495e-09
- gate_up_grad: bfloat16 [2, 4096, 14336], P(None, 'fsdp', ('rep', 'tp')), may hold values from -8 to 8
- down_master: float32 [4096, 14336], P('fsdp', ('rep', 'tp')), may hold values from -0.046875 to 0.046875
- down_moment: float32 [4096, 14336], P('fsdp', ('rep', 'tp')), may hold values from -0.00018310547 to 0.00018310547
- down_second: float32 [4096, 14336], P('fsdp', ('rep', 'tp')), may hold values from 8.5149493e-10 to 8.51495e-09
- down_grad: bfloat16 [4096, 14336], P('fsdp', ('rep', 'tp')), may hold values from -8 to 8
- norm_gain: float32 [4096], replicated, may hold values from 0.1 to 1.9
- start_rows: bfloat16 [256, 4096], P(('rep', 'fsdp', 'tp')), may hold values from -6 to 6
- queries: bfloat16 [2, 256, 4096], P(None, ('rep', 'fsdp', 'tp')), may hold values from -6 to 6
- new_kv: bfloat16 [2, 256, 2, 1024], P(None, ('rep', 'fsdp', 'tp')), may hold values from -6 to 6
- kv_pool: bfloat16 [2048, 16, 2, 1024], P(('rep', 'fsdp', 'tp')), may hold values from -6 to 6
- page_table: int32 [256, 8], P(('rep', 'fsdp', 'tp')), may hold values from 0 to 63, as said below
- cache_len: int32 [256], P(('rep', 'fsdp', 'tp')), may hold values from 1 to 128, as said below
Outputs:
- final_rows: bfloat16 [256, 4096], P(('rep', 'fsdp', 'tp'))
Inputs may be any that keep to these rules, and one draw needn't show every extreme that they name: `page_table`: within each aligned block of 8 rows, the entries name each of the 64 pages of that block exactly once. `cache_len`: some row has exactly 128 cached positions.
All inputs are finite; a program needn't handle non-finite values.
Results may differ from a plain program's by a relative error of at most 0.019.
Values may be sent and summed in bfloat16 or wider, within the bound.
A program may use at most 192 MiB of HBM per device.

v0:
```python
import jax
import jax.numpy as jnp
from jax import lax
from jax.sharding import PartitionSpec as P

D = 4096
HD = 128


beta_one = 0.9
beta_two = 0.95
adam_eps = 1e-08
adam_time = 100.0
norm_eps = 1e-05


def adam_new(master, moment, second, grad, clip):
    learn_rate = 2.0 / D**0.5
    g = grad.astype(jnp.float32) * clip
    m = beta_one * moment + (1.0 - beta_one) * g
    v = beta_two * second + (1.0 - beta_two) * g * g
    first_fix = 1.0 - beta_one**adam_time
    second_fix = 1.0 - beta_two**adam_time
    return (master - learn_rate * (m / first_fix) / (jnp.sqrt(v / second_fix) + adam_eps)).astype(
        jnp.bfloat16
    )


def attend(query, keys, values, valid, fresh_k, fresh_v, step):
    scale = query.shape[-1] ** (-0.5)
    old = jnp.einsum("rjgh,rcjh->rjgc", query, keys, preferred_element_type=jnp.float32) * scale
    old = jnp.where(valid[:, None, None, :], old, -1e30)
    new = jnp.einsum("rjgh,srjh->rjgs", query, fresh_k, preferred_element_type=jnp.float32) * scale
    allowed = jnp.arange(fresh_k.shape[0]) <= step
    new = jnp.where(allowed[None, None, None, :], new, -1e30)
    top = jnp.maximum(jnp.max(old, axis=-1, keepdims=True), jnp.max(new, axis=-1, keepdims=True))
    exp_old = jnp.exp(old - top)
    exp_new = jnp.exp(new - top)
    total = jnp.sum(exp_old, axis=-1, keepdims=True) + jnp.sum(exp_new, axis=-1, keepdims=True)
    prob_old = (exp_old / total).astype(jnp.bfloat16)
    prob_new = (exp_new / total).astype(jnp.bfloat16)
    out = jnp.einsum("rjgc,rcjh->rjgh", prob_old, values, preferred_element_type=jnp.float32)
    out = out + jnp.einsum("rjgs,srjh->rjgh", prob_new, fresh_v, preferred_element_type=jnp.float32)
    return out.reshape(out.shape[0], -1)


def shards(
    gate_up_master,
    gate_up_moment,
    gate_up_second,
    gate_up_grad,
    down_master,
    down_moment,
    down_second,
    down_grad,
    norm_gain,
    start_rows,
    queries,
    new_kv,
    kv_pool,
    page_table,
    cache_len,
):
    local_squares = jnp.sum(jnp.square(gate_up_grad.astype(jnp.float32))) + jnp.sum(
        jnp.square(down_grad.astype(jnp.float32))
    )
    total = lax.psum(local_squares, ("rep", "fsdp", "tp"))
    clip = jnp.minimum(1.0, 1.0 / jnp.sqrt(total))
    gate_up = adam_new(gate_up_master, gate_up_moment, gate_up_second, gate_up_grad, clip)
    down_t = adam_new(down_master, down_moment, down_second, down_grad, clip)[None]
    n_fsdp = lax.axis_size("fsdp")
    n_rep = lax.axis_size("rep")
    cols = gate_up.shape[2]
    copied = (
        lax.all_gather(gate_up, "rep", axis=2, tiled=True),
        lax.all_gather(down_t, "rep", axis=2, tiled=True),
    )
    shaped = tuple(
        (a.reshape(a.shape[0], a.shape[1], n_rep, n_fsdp, cols // n_fsdp) for a in copied)
    )
    moved = (
        lax.all_to_all(shaped[0], "fsdp", split_axis=3, concat_axis=1, tiled=True),
        lax.all_to_all(shaped[1], "fsdp", split_axis=3, concat_axis=1, tiled=True),
    )
    weights = tuple((a.reshape(a.shape[0], a.shape[1], -1) for a in moved))
    roll_gate_up = weights[0]
    roll_down = weights[1][0]
    local_rows = start_rows.shape[0]
    kv_width = new_kv.shape[-1]
    head_dim = HD
    key_heads = kv_width // head_dim
    cache = kv_pool[page_table].reshape(local_rows, -1, 2, key_heads, head_dim)
    keys = cache[:, :, 0]
    values = cache[:, :, 1]
    valid = jnp.arange(keys.shape[1], dtype=jnp.int32)[None, :] < cache_len[:, None]
    fresh = new_kv.reshape(new_kv.shape[0], local_rows, 2, key_heads, head_dim)
    fresh_k = fresh[:, :, 0]
    fresh_v = fresh[:, :, 1]
    rows = start_rows
    for step in range(queries.shape[0]):
        query = queries[step].reshape(local_rows, key_heads, -1, head_dim)
        attended = attend(query, keys, values, valid, fresh_k, fresh_v, step)
        mixed = (rows.astype(jnp.float32) + attended).astype(jnp.bfloat16)
        mixed_f = mixed.astype(jnp.float32)
        normed = (
            mixed_f
            * lax.rsqrt(jnp.mean(mixed_f * mixed_f, axis=-1, keepdims=True) + norm_eps)
            * norm_gain
        ).astype(jnp.bfloat16)
        whole = lax.all_gather(normed, ("fsdp", "tp"), axis=0, tiled=True)
        gate = jnp.dot(whole, roll_gate_up[0], preferred_element_type=jnp.float32)
        upper = jnp.dot(whole, roll_gate_up[1], preferred_element_type=jnp.float32)
        hidden = (jax.nn.silu(gate) * upper).astype(jnp.bfloat16)
        summed = lax.psum_scatter(
            lax.dot_general(
                hidden, roll_down, (((1,), (1,)), ((), ())), preferred_element_type=jnp.float32
            ),
            ("fsdp", "tp"),
            scatter_dimension=0,
            tiled=True,
        )
        rows = (mixed_f + summed).astype(jnp.bfloat16)
    return rows


def solution(mesh):
    in_specs = (
        P(None, "fsdp", ("rep", "tp")),
        P(None, "fsdp", ("rep", "tp")),
        P(None, "fsdp", ("rep", "tp")),
        P(None, "fsdp", ("rep", "tp")),
        P("fsdp", ("rep", "tp")),
        P("fsdp", ("rep", "tp")),
        P("fsdp", ("rep", "tp")),
        P("fsdp", ("rep", "tp")),
        P(),
        P(("rep", "fsdp", "tp"), None),
        P(None, ("rep", "fsdp", "tp"), None),
        P(None, ("rep", "fsdp", "tp"), None, None),
        P(("rep", "fsdp", "tp"), None, None, None),
        P(("rep", "fsdp", "tp"), None),
        P(("rep", "fsdp", "tp")),
    )
    out_specs = P(("rep", "fsdp", "tp"), None)
    return jax.shard_map(shards, mesh=mesh, in_specs=in_specs, out_specs=out_specs, check_vma=False)
```

profile of v0, /device:TPU:0, one launch (start us, length us, event | category | flops | bytes accessed | tf_op | source)
XLA Modules:
  0.0 831.0 jit_solution(12669053569953557174)
XLA Ops:
  7.4 5.9 copy.41
  13.3 4.5 fusion.16
  17.8 9.9 %copy.40 = bf16[2,1024,1792]{1,2,0:T(8,128)(2,1)} copy(bf16[2,1024,1792]{2,1,0:T(8,128)(2,1)} %param.18) | data formatting | bytes 14680064 | tf_op args[3]
  27.8 7.5 fusion.5
  36.4 42.0 %psum.7 = f32[]{:T(128)} all-reduce(f32[]{:T(128)S(6)} %add.102), channel_id=1, replica_groups=mesh['rep'=2,'fsdp'=4,'tp'=4] {'rep','fsdp','tp'}, use_global_device_ids=true, to_apply=%region_7.8 | all-reduce | flops 1 | bytes 8 | tf_op jit(solution)/shard_map/psum | solution.py:67
  79.2 8.4 %copy.49 = f32[1024,1792]{0,1:T(8,128)} copy(f32[1024,1792]{1,0:T(8,128)} %param.19) | data formatting | bytes 14680064 | tf_op args[4]
  87.6 8.4 %copy.47 = f32[1024,1792]{0,1:T(8,128)} copy(f32[1024,1792]{1,0:T(8,128)} %param.20) | data formatting | bytes 14680064 | tf_op args[5]
  95.9 8.4 %copy.48 = f32[1024,1792]{0,1:T(8,128)} copy(f32[1024,1792]{1,0:T(8,128)} %param.21) | data formatting | bytes 14680064 | tf_op args[6]
  104.3 12.5 %fusion.21 = bf16[1024,1792]{0,1:T(8,128)(2,1)} fusion(f32[1024,1792]{0,1:T(8,128)} %copy.49, f32[1024,1792]{0,1:T(8,128)} %copy.48, bf16[1024,1792]{0,1:T(8,128)(2,1)} %copy.41, f32[1024,1792]{0,1:T(8,128)} %copy.47, f32[]{:T(128)S(6)} %min.3), kind=kLoop, calls=%fused_computation.28 | loop fusion | flops 27525120 | bytes 29360132 | tf_op jit(solution)/shard_map/convert_element_type | solution.py:24
  117.1 14.8 %copy.43 = f32[2,1024,1792]{1,2,0:T(8,128)} copy(f32[2,1024,1792]{2,1,0:T(8,128)} %param.15) | data formatting | bytes 29360128 | tf_op args[0]
  131.9 14.5 %copy.39 = f32[2,1024,1792]{1,2,0:T(8,128)} copy(f32[2,1024,1792]{2,1,0:T(8,128)} %param.16) | data formatting | bytes 29360128 | tf_op args[1]
  146.5 14.3 %copy.42 = f32[2,1024,1792]{1,2,0:T(8,128)} copy(f32[2,1024,1792]{2,1,0:T(8,128)} %param.17) | data formatting | bytes 29360128 | tf_op args[2]
  160.7 21.6 %fusion.10 = bf16[2,1024,1792]{1,2,0:T(8,128)(2,1)} fusion(f32[2,1024,1792]{1,2,0:T(8,128)} %copy.43, f32[2,1024,1792]{1,2,0:T(8,128)} %copy.42, bf16[2,1024,1792]{1,2,0:T(8,128)(2,1)} %copy.40, f32[2,1024,1792]{1,2,0:T(8,128)} %copy.39, f32[]{:T(128)S(6)} %min.3), kind=kLoop, calls=%fused_computation.14 | loop fusion | flops 55050240 | bytes 58720260 | tf_op jit(solution)/shard_map/convert_element_type | solution.py:24
  182.3 26.8 %all-gather.12.cloned.1.call-done = bf16[1024,3584]{0,1:T(8,128)(2,1)} async-done(((bf16[1024,1792]{0,1:T(8,128)(2,1)}), bf16[1024,3584]{0,1:T(8,128)(2,1)}) %all-gather.12.cloned.1.call-update) | async-done | bytes 7340048 | tf_op jit(solution)/shard_map/all_gather | solution.py:76
  209.2 6.9 copy.50
  216.1 6.1 all-to-all-start.1
  222.2 163.8 %all-gather.8.cloned.1.call-done = bf16[2,1024,3584]{1,2,0:T(8,128)(2,1)} async-done(((bf16[2,1024,1792]{1,2,0:T(8,128)(2,1)}), bf16[2,1024,3584]{1,2,0:T(8,128)(2,1)}) %all-gather.8.cloned.1.call-update) | async-done | bytes 14680080 | tf_op jit(solution)/shard_map/all_gather | solution.py:75
  385.9 13.4 %copy.44 = bf16[2,1024,2,4,448]{1,4,2,0,3:T(8,128)(2,1)} copy(bf16[2,1024,2,4,448]{1,4,3,2,0:T(8,128)(2,1)} %bitcast.90) | data formatting | bytes 29360128 | tf_op jit(solution)/shard_map/reshape | solution.py:79
  399.4 6.8 all-to-all-start
  406.5 12.9 %gather_fusion = bf16[64,16,2,1024]{3,2,1,0:T(2,128)(2,1)} fusion(bf16[64,16,2,1024]{3,2,1,0:T(2,128)(2,1)} %param.27, s32[1024]{0:T(1024)S(1)} %pad_clamp_fusion), kind=kCustom, calls=%fused_computation | custom fusion | bytes 8388864 | tf_op jit(solution)/shard_map/gather | solution.py:92
  419.4 7.6 reshape.110
  427.4 2.5 fusion.73
  429.9 1.3 copy-done.2
  431.2 1.3 fusion.78
  432.9 0.3 fusion.68
  433.1 0.7 fusion.28
  434.1 0.7 fusion.54
  434.8 0.4 reduce-scatter.3.cloned.1.call-start
  435.3 11.8 %copy.51 = bf16[1,4,1024,2,1,448]{2,1,5,3,4,0:T(4,128)(2,1)} copy(bf16[1,4,1024,2,1,448]{2,5,3,1,4,0:T(8,128)(2,1)} %bitcast.11) | data formatting | bytes 14680064 | tf_op jit(solution)/shard_map/all_to_all | solution.py:83
  447.1 10.9 %copy.64 = bf16[112,8,4,1024]{3,1,2,0:T(8,128)(2,1)} copy(bf16[112,8,4,1024]{3,2,1,0:T(4,128)(2,1)} %bitcast.87) | data formatting | bytes 14680064
  457.9 112.3 %all-to-all-done = bf16[2,1024,2,4,448]{1,4,2,0,3:T(8,128)(2,1)} async-done(((bf16[2,1024,2,4,448]{1,4,2,0,3:T(8,128)(2,1)}), bf16[2,1024,2,4,448]{1,4,2,0,3:T(8,128)(2,1)}, u32[]{:S(2)}, u32[]{:S(2)}) %all-to-all-start) | async-done | bytes 14680096 | tf_op jit(solution)/shard_map/all_to_all | solution.py:82
  570.3 10.7 %fusion.72 = (bf16[1,4,1024,2,1,448]{2,5,3,0,1,4:T(8,128)(2,1)}, bf16[1,4,1024,2,1,448]{2,5,3,0,1,4:T(8,128)(2,1)}) fusion(bf16[2,4,1024,2,1,448]{2,5,3,0,1,4:T(8,128)(2,1)} %bitcast.7), kind=kLoop, calls=%fused_computation.110 | loop fusion | bytes 29360128 | tf_op jit(solution)/shard_map/slice | solution.py:111
  581.0 11.7 %copy.45 = bf16[1,4,1024,2,1,448]{2,1,5,3,4,0:T(4,128)(2,1)} copy(bf16[1,4,1024,2,1,448]{2,5,3,0,1,4:T(8,128)(2,1)} %get-tuple-element.9) | data formatting | bytes 14680064 | tf_op jit(solution)/shard_map/slice | solution.py:111
  592.7 10.9 %copy.62 = bf16[112,8,4,1024]{3,1,2,0:T(8,128)(2,1)} copy(bf16[112,8,4,1024]{3,2,1,0:T(4,128)(2,1)} %bitcast.88) | data formatting | bytes 14680064
  603.6 11.9 %copy.46 = bf16[1,4,1024,2,1,448]{2,1,5,3,4,0:T(4,128)(2,1)} copy(bf16[1,4,1024,2,1,448]{2,5,3,0,1,4:T(8,128)(2,1)} %get-tuple-element.10) | data formatting | bytes 14680064 | tf_op jit(solution)/shard_map/slice | solution.py:112
  615.5 10.9 %copy.63 = bf16[112,8,4,1024]{3,1,2,0:T(8,128)(2,1)} copy(bf16[112,8,4,1024]{3,2,1,0:T(4,128)(2,1)} %bitcast.89) | data formatting | bytes 14680064
  626.4 6.7 fusion.80
  633.1 11.0 %fusion.39 = f32[128,4096]{1,0:T(8,128)} fusion(bf16[4096,896]{0,1:T(8,128)(2,1)} %bitcast.81, bf16[128,4096]{1,0:T(8,128)(2,1)S(1)} %copy-done, bf16[4096,896]{0,1:T(8,128)(2,1)} %bitcast.85, f32[128,896]{1,0:T(8,128)} %fusion.80), kind=kOutput, calls=%fused_computation.52 | convolution fusion | flops 1879736320 | bytes 18284544 | tf_op jit(solution)/shard_map/dot_general | solution.py:115
  644.5 2.9 fusion.76
  648.1 0.7 fusion.29
  648.9 56.0 %reduce-scatter.3.cloned.1.call-done = f32[8,4096]{1,0:T(8,128)} async-done(((f32[128,4096]{1,0:T(8,128)}), f32[8,4096]{1,0:T(8,128)}) %reduce-scatter.3.cloned.1.call-update) | async-done | bytes 131088 | tf_op jit(solution)/shard_map/reduce_scatter | solution.py:114
  704.9 1.1 fusion.56
  705.9 0.7 fusion.58
  706.7 37.5 %all-gather.10.cloned.1.call-done = bf16[128,4096]{1,0:T(8,128)(2,1)} async-done(((bf16[8,4096]{1,0:T(8,128)(2,1)}), bf16[128,4096]{1,0:T(8,128)(2,1)}) %all-gather.10.cloned.1.call-update) | async-done | bytes 1048592 | tf_op jit(solution)/shard_map/all_gather | solution.py:110
  744.2 5.9 fusion.81
  750.1 10.6 %fusion.38 = f32[128,4096]{1,0:T(8,128)} fusion(bf16[4096,896]{0,1:T(8,128)(2,1)} %bitcast.82, bf16[128,4096]{1,0:T(8,128)(2,1)S(1)} %copy-done.1, bf16[4096,896]{0,1:T(8,128)(2,1)} %bitcast.86, f32[128,896]{1,0:T(8,128)S(1)} %fusion.81), kind=kOutput, calls=%fused_computation.51 | convolution fusion | flops 1879736320 | bytes 18284544 | tf_op jit(solution)/shard_map/dot_general | solution.py:115
  760.8 60.6 %reduce-scatter.5.cloned.1.call-done = f32[8,4096]{1,0:T(8,128)} async-done(((f32[128,4096]{1,0:T(8,128)}), f32[8,4096]{1,0:T(8,128)}) %reduce-scatter.5.cloned.1.call-update) | async-done | bytes 131088 | tf_op jit(solution)/shard_map/reduce_scatter | solution.py:114
  821.4 1.5 fusion.59
  (57 shorter events, 2.7 us)
Async XLA Ops:
  7.4 201.8 %all-gather.12.cloned.1.call-start = ((), (), s32[]{:S(2)}) async-start(), calls=%async_computation.9 | async-start | bytes 11010048 | tf_op jit(solution)/shard_map/all_gather | solution.py:76
  116.8 269.1 %all-gather.8.cloned.1.call-start = ((), (), s32[]{:S(2)}) async-start(), calls=%async_computation.5 | async-start | bytes 22020096 | tf_op jit(solution)/shard_map/all_gather | solution.py:75
  216.1 183.3 %all-to-all-start.1 = ((bf16[1,1024,2,4,448]{1,4,2,0,3:T(8,128)(2,1)}), bf16[1,1024,2,4,448]{1,4,2,0,3:T(8,128)(2,1)}, u32[]{:S(2)}, u32[]{:S(2)}) async-start(bf16[1,1024,2,4,448]{1,4,2,0,3:T(8,128)(2,1)} %copy.50), calls=%async_computation.1 | async-start | bytes 14680064 | tf_op jit(solution)/shard_map/all_to_all | solution.py:83
  399.4 6.9 copy-start.7
  399.4 7.0 copy-start.5
  399.4 7.0 copy-start.3
  399.4 170.9 %all-to-all-start = ((bf16[2,1024,2,4,448]{1,4,2,0,3:T(8,128)(2,1)}), bf16[2,1024,2,4,448]{1,4,2,0,3:T(8,128)(2,1)}, u32[]{:S(2)}, u32[]{:S(2)}) async-start(bf16[2,1024,2,4,448]{1,4,2,0,3:T(8,128)(2,1)} %copy.44), calls=%async_computation | async-start | bytes 29360128 | tf_op jit(solution)/shard_map/all_to_all | solution.py:82
  406.2 220.2 %all-gather.6.cloned.1.call-start = ((), (), s32[]{:S(2)}) async-start(), calls=%async_computation.4 | async-start | bytes 1114112 | tf_op jit(solution)/shard_map/all_gather | solution.py:110
  406.5 20.5 %copy-start.8 = (s32[8]{0:T(128)S(1)}, s32[8]{0:T(128)}, u32[]{:S(2)}) copy-start(s32[8]{0:T(128)} %param.29) | copy-start | bytes 100
  427.3 6.6 copy-start.6
  427.3 6.8 copy-start.4
  429.9 1.3 copy-start.2
  434.8 270.0 %reduce-scatter.3.cloned.1.call-start = ((), (), s32[]{:S(2)}) async-start(), calls=%async_computation.6 | async-start | bytes 2228224 | tf_op jit(solution)/shard_map/reduce_scatter | solution.py:114
  626.4 6.7 copy-start
  644.1 100.1 %all-gather.10.cloned.1.call-start = ((), (), s32[]{:S(2)}) async-start(), calls=%async_computation.7 | async-start | bytes 1114112 | tf_op jit(solution)/shard_map/all_gather | solution.py:110
  706.7 114.8 %reduce-scatter.5.cloned.1.call-start = ((), (), s32[]{:S(2)}) async-start(), calls=%async_computation.8 | async-start | bytes 2228224 | tf_op jit(solution)/shard_map/reduce_scatter | solution.py:114
  744.2 5.9 copy-start.1
Sparse Core Ops, SparseCore 0:
  116.9 92.1 all-gather.11
  210.7 175.1 all-gather.7
Sparse Core Ops, SparseCore 1:
  434.9 40.3 all-gather.5
  644.2 60.6 reduce-scatter.2
  707.2 36.9 all-gather.9
  760.9 60.5 reduce-scatter.4
where the time goes:
time: 840 us; the launch traced here: 831 us
  waiting for transfers between devices  457 us (54%)
  local copies, waits for them, and re-layouts  208 us (25%)
  other arithmetic  51.2 us (6%)
  blocking collectives  42 us (5%)
  matrix products  40.8 us (5%)
  between operations  17.7 us (2%)
  starting transfers between devices  13.7 us (2%)
    all_gather x1, waiting for transfers between devices, shards(): lax.all_gather(gate_up, 'rep', axis=2, tiled=True)  164 us
    unnamed x29, local copies, waits for them, and re-layouts  119 us
    reduce_scatter x2, waiting for transfers between devices, shards(): lax.psum_scatter(lax.dot_general(hidden, roll_down, (((1,), (1,)), ((), (...  117 us
    all_to_all x1, waiting for transfers between devices, shards(): lax.all_to_all(shaped[0], 'fsdp', split_axis=3, concat_axis=1, tiled=True)  112 us
    psum x1, blocking collectives, shards(): total = lax.psum(local_squares, ('rep', 'fsdp', 'tp'))  42 us
    all_gather x2, waiting for transfers between devices, shards(): whole = lax.all_gather(normed, ('fsdp', 'tp'), axis=0, tiled=True)  37.5 us
    convert_element_type x2, other arithmetic, adam_new(): (master - learn_rate * (m / first_fix) / (jnp.sqrt(v / second_fix) + adam...  34 us
    all_gather x1, waiting for transfers between devices, shards(): lax.all_gather(down_t, 'rep', axis=2, tiled=True)  26.8 us
  transfers between devices with their start and end apart: 8, of which 6 were waited for; matrix products, arithmetic and copies ran while one was open for 24% of the time, Pallas kernels for 0%

commit v1 on v0

v1 whole, which is shorter than its diff:
```python
import functools

import jax
import jax.numpy as jnp
from jax import lax
from jax.experimental import pallas as pl
from jax.experimental.pallas import tpu as pltpu
from jax.sharding import PartitionSpec as P

HD = 128
FULL_WIDTH = 4096
MESH = pl.DeviceIdType.MESH

beta_one = 0.9
beta_two = 0.95
adam_eps = 1e-08
adam_time = 100.0
norm_eps = 1e-05

TILE = 256
CHUNK = 128
SUB = 16
SLOTS = 4


def attend_all(queries, kv_pool, page_table, cache_len, new_kv):
    steps, rows, _ = queries.shape
    pages, page, _, kv_width = kv_pool.shape
    heads = kv_width // HD
    scale = HD**-0.5
    pool = kv_pool.reshape(pages * page, 2, heads, HD)
    keys, values = pool[:, 0], pool[:, 1]
    slot = jnp.arange(page_table.shape[1], dtype=jnp.int32) * page
    place = slot[None, :, None, None] + jnp.arange(page, dtype=jnp.int32)
    named = page_table[:, :, None] == jnp.arange(pages, dtype=jnp.int32)
    valid = named[..., None] & (place < cache_len[:, None, None, None])
    valid = jnp.any(valid, axis=1).reshape(rows, pages * page)
    fresh = new_kv.reshape(steps, rows, 2, heads, HD)
    fresh_k, fresh_v = fresh[:, :, 0], fresh[:, :, 1]
    query = queries.reshape(steps, rows, heads, -1, HD)
    old = jnp.einsum("srjgh,cjh->jsrgc", query, keys, preferred_element_type=jnp.float32) * scale
    old = jnp.where(valid[None, None, :, None, :], old, -1e30)
    new = jnp.einsum("srjgh,trjh->jsrgt", query, fresh_k, preferred_element_type=jnp.float32) * scale
    allowed = jnp.arange(steps)[None, :] <= jnp.arange(steps)[:, None]
    new = jnp.where(allowed[None, :, None, None, :], new, -1e30)
    top = jnp.maximum(jnp.max(old, axis=-1, keepdims=True), jnp.max(new, axis=-1, keepdims=True))
    exp_old = jnp.exp(old - top)
    exp_new = jnp.exp(new - top)
    total = jnp.sum(exp_old, axis=-1, keepdims=True) + jnp.sum(exp_new, axis=-1, keepdims=True)
    prob_old = (exp_old / total).astype(jnp.bfloat16)
    prob_new = (exp_new / total).astype(jnp.bfloat16)
    out = jnp.einsum("jsrgc,cjh->srjgh", prob_old, values, preferred_element_type=jnp.float32)
    out = out + jnp.einsum("jsrgt,trjh->srjgh", prob_new, fresh_v, preferred_element_type=jnp.float32)
    return out.reshape(steps, rows, -1)


def block_kernel(
    n_rep,
    n_fsdp,
    n_tp,
    gu_master,
    gu_moment,
    gu_second,
    gu_grad,
    d_master,
    d_moment,
    d_second,
    d_grad,
    pieces,
    gain,
    out,
    weights,
    slots,
    got_pieces,
    sums,
    x,
    own,
    core_out,
    core_in,
    y_out,
    y_in,
    hid,
    acc,
    down_out,
    down_in,
    squares,
    mixed,
    fin_out,
    fin_in,
    grad_sem,
    slot_sem,
    f_send,
    f_recv,
    s_send,
    s_recv,
    x_send,
    x_recv,
    core_send,
    core_recv,
    y_send,
    y_recv,
    h_send,
    h_recv,
    hc_send,
    hc_recv,
    d_send,
    d_recv,
):
    n_group = n_rep * n_tp
    members = n_fsdp // 2
    depth, cols = d_grad.shape
    tiles = cols // TILE
    steps = pieces.shape[1] // 8 - 1
    half = x.shape[1] * x.shape[2]
    part = half // members

    r = lax.axis_index("rep")
    f = lax.axis_index("fsdp")
    t = lax.axis_index("tp")
    g = r * n_tp + t
    c = lax.rem(f, 2)
    m = f // 2

    def f_dev(k):
        return (r, lax.rem(f + k, n_fsdp), t)

    def g_dev(k):
        there = lax.rem(g + k, n_group)
        return (there // n_tp, f, lax.rem(there, n_tp))

    def m_dev(k):
        return (r, lax.rem(m + k, members) * 2 + c, t)

    sibling = (r, m * 2 + 1 - c, t)

    barrier = pltpu.get_barrier_semaphore()
    for k in range(1, n_fsdp):
        pl.semaphore_signal(barrier, inc=1, device_id=f_dev(k), device_id_type=MESH)
    for k in range(1, n_group):
        pl.semaphore_signal(barrier, inc=1, device_id=g_dev(k), device_id_type=MESH)

    stacks = (
        (gu_master.at[0], gu_moment.at[0], gu_second.at[0], gu_grad.at[0]),
        (gu_master.at[1], gu_moment.at[1], gu_second.at[1], gu_grad.at[1]),
        (d_master, d_moment, d_second, d_grad),
    )
    per = depth // CHUNK
    chunks = [(s, i) for s in range(3) for i in range(per)]

    def grad_copy(n):
        s, i = chunks[n]
        rows = pl.ds(i * CHUNK, CHUNK)
        return pltpu.make_async_copy(stacks[s][3].at[rows], weights.at[s, rows], grad_sem.at[n])

    def state_copies(n):
        s, i = chunks[n]
        rows = pl.ds(i * CHUNK, CHUNK)
        slot = n % SLOTS
        return [
            pltpu.make_async_copy(stacks[s][a].at[rows], slots.at[slot, a], slot_sem.at[slot, a])
            for a in range(3)
        ]

    for n in range(len(chunks)):
        grad_copy(n).start()
    for n in range(min(SLOTS, len(chunks))):
        for copy in state_copies(n):
            copy.start()

    pl.semaphore_wait(barrier, n_fsdp + n_group - 2)

    def remote(src, dst, send, recv, dev):
        return pltpu.make_async_remote_copy(
            src_ref=src, dst_ref=dst, send_sem=send, recv_sem=recv, device_id=dev, device_id_type=MESH
        )

    piece_copies = []
    for k in range(1, n_fsdp):
        there = lax.rem(f + k, n_fsdp)
        copy = remote(pieces.at[there], got_pieces.at[k], f_send.at[k], f_recv.at[k], f_dev(k))
        copy.start()
        piece_copies.append(copy)
    got_pieces[0] = pieces[f]

    total = jnp.zeros((8, cols), jnp.float32)
    for n in range(len(chunks)):
        grad_copy(n).wait()
        s, i = chunks[n]

        def square(b, run, s=s, i=i):
            rows = pl.ds(pl.multiple_of(i * CHUNK + b * SUB, SUB), SUB)
            v = weights[s, rows, :].astype(jnp.float32)
            v = v * v
            return run + (v[:8] + v[8:])

        total = lax.fori_loop(0, CHUNK // SUB, square, total)
    tile_sum = total[:, :128]
    for b in range(1, cols // 128):
        tile_sum = tile_sum + total[:, b * 128 : (b + 1) * 128]

    def sum_over(value, base, n, dev):
        sums[base] = value
        copies = []
        for k in range(1, n):
            copy = remote(sums.at[base], sums.at[base + k], s_send.at[base + k], s_recv.at[base + k], dev(k))
            copy.start()
            copies.append(copy)
        for copy in copies:
            copy.wait()
        for k in range(1, n):
            value = value + sums[base + k]
        return value

    tile_sum = sum_over(tile_sum, 0, n_fsdp, f_dev)

    for copy in piece_copies:
        copy.wait()

    def piece(a):
        blocks = [None] * n_fsdp
        at = pl.ds(a * 8, 8)
        for k in range(n_fsdp):
            blocks[k] = got_pieces[lax.rem(f - k + n_fsdp, n_fsdp), at, :]
        return jnp.concatenate(blocks, axis=0)

    x[0, 0] = piece(0).astype(jnp.bfloat16)
    mixed[...] = piece(1)

    def send_x():
        copies = []
        for k in range(1, n_group):
            at = x.at[k // x.shape[1], k % x.shape[1]]
            copy = remote(x.at[0, 0], at, x_send.at[k], x_recv.at[k], g_dev(k))
            copy.start()
            copies.append(copy)
        return copies

    tile_sum = sum_over(tile_sum, n_fsdp, n_group, g_dev)
    x_copies = send_x()
    clip = jnp.minimum(1.0, lax.rsqrt(jnp.sum(tile_sum, keepdims=True)))

    rate = 2.0 / FULL_WIDTH**0.5 / (1.0 - beta_one**adam_time)
    keep_m = rate * beta_one
    add_m = rate * (1.0 - beta_one)
    second_fix = 1.0 - beta_two**adam_time
    keep_v = beta_two / second_fix
    add_v = (1.0 - beta_two) / second_fix
    for n in range(len(chunks)):
        s, i = chunks[n]
        slot = n % SLOTS
        for copy in state_copies(n):
            copy.wait()

        def update(b, carry, s=s, i=i, slot=slot):
            at = pl.ds(pl.multiple_of(b * SUB, SUB), SUB)
            rows = pl.ds(pl.multiple_of(i * CHUNK + b * SUB, SUB), SUB)
            grad = weights[s, rows, :].astype(jnp.float32) * clip
            first = keep_m * slots[slot, 1, at, :] + add_m * grad
            second = keep_v * slots[slot, 2, at, :] + add_v * (grad * grad)
            new = slots[slot, 0, at, :] - first / (jnp.sqrt(second) + adam_eps)
            weights[s, rows, :] = new.astype(jnp.bfloat16)
            return carry

        lax.fori_loop(0, CHUNK // SUB, update, 0)
        if n + SLOTS < len(chunks):
            for copy in state_copies(n + SLOTS):
                copy.start()

    for copy in x_copies:
        copy.wait()

    for step in range(steps):

        def core_copy(j):
            return remote(core_out.at[j], core_in.at[j], core_send.at[j], core_recv.at[j], sibling)

        def y_copy(j, k):
            there = lax.rem(m + k, members)
            return remote(
                y_out.at[j, there], y_in.at[j, k - 1], y_send.at[j, k - 1], y_recv.at[j, k - 1], m_dev(k)
            )

        def h_copy(j, k):
            return remote(
                hid.at[j, c, m], hid.at[j, c, m], h_send.at[j, k - 1], h_recv.at[j, k - 1], m_dev(k)
            )

        def h_arrival(j, k):
            there = lax.rem(m - k + members, members)
            return remote(
                hid.at[j, c, m], hid.at[j, c, there], h_send.at[j, k - 1], h_recv.at[j, k - 1], m_dev(k)
            )

        def hc_copy(j):
            return remote(hid.at[j, c], hid.at[j, c], hc_send.at[j], hc_recv.at[j], sibling)

        def hc_arrival(j):
            return remote(hid.at[j, c], hid.at[j, 1 - c], hc_send.at[j], hc_recv.at[j], sibling)

        def multiply(j):
            at = pl.ds(pl.multiple_of(j * TILE, TILE), TILE)
            theirs = x[1 - c].reshape(half, depth)
            mine = x[c].reshape(half, depth)
            both = jnp.concatenate([theirs, mine], axis=0)
            for a in range(2):
                y = jnp.dot(both, weights[a, :, at], preferred_element_type=jnp.float32)
                core_out[j, :, a * TILE : (a + 1) * TILE] = y[:half].astype(jnp.bfloat16)
                own[j, :, a * TILE : (a + 1) * TILE] = y[half:]
            core_copy(j).start()

        def add_core(j):
            core_copy(j).wait()
            y = own[j] + core_in[j].astype(jnp.float32)
            own[j] = y
            y_out[j] = y.astype(jnp.bfloat16).reshape(members, part, 2 * TILE)
            for k in range(1, members):
                y_copy(j, k).start()

        def first_stage(j, carry):
            multiply(j)

            @pl.when(j > 0)
            def _():
                add_core(j - 1)

            return carry

        lax.fori_loop(0, tiles, first_stage, 0)
        add_core(tiles - 1)

        def second_stage(j, carry):
            y = own[j, pl.ds(pl.multiple_of(m * part, part), part), :]
            for k in range(1, members):
                y_copy(j, k).wait()
                y = y + y_in[j, k - 1].astype(jnp.float32)
            gate, upper = y[:, :TILE], y[:, TILE:]
            hid[j, c, m] = (gate * jax.nn.sigmoid(gate) * upper).astype(jnp.bfloat16)
            for k in range(1, members):
                h_copy(j, k).start()
            return carry

        lax.fori_loop(0, tiles, second_stage, 0)

        def third_stage(j, carry):
            for k in range(1, members):
                h_copy(j, k).wait_send()
                h_arrival(j, k).wait_recv()
            hc_copy(j).start()
            return carry

        lax.fori_loop(0, tiles, third_stage, 0)

        acc[...] = jnp.zeros_like(acc)

        def fourth_stage(j, carry):
            hc_copy(j).wait_send()
            hc_arrival(j).wait_recv()
            at = pl.ds(pl.multiple_of(j * TILE, TILE), TILE)
            acc[...] += lax.dot_general(
                hid[j].reshape(2 * half, TILE),
                weights[2, :, at],
                (((1,), (1,)), ((), ())),
                preferred_element_type=jnp.float32,
            )
            return carry

        lax.fori_loop(0, tiles, fourth_stage, 0)

        rows_of = acc.shape[0] // n_group
        copies = []
        for k in range(1, n_group):
            down_out[k] = acc[k * rows_of : (k + 1) * rows_of, :].astype(jnp.bfloat16)
            copy = remote(
                down_out.at[k], down_in.at[k], d_send.at[k], d_recv.at[k], g_dev(n_group - k)
            )
            copy.start()
            copies.append(copy)
        summed = acc[:rows_of, :]
        for k in range(1, n_group):
            copies[k - 1].wait()
            summed = summed + down_in[k].astype(jnp.float32)
        rows = (mixed[...] + summed).astype(jnp.bfloat16).astype(jnp.float32)

        if step < steps - 1:
            blend = (rows + piece(2 + step)).astype(jnp.bfloat16).astype(jnp.float32)
            mixed[...] = blend
            local = jnp.sum(blend * blend, axis=1, keepdims=True)
            squares[0] = jnp.broadcast_to(local, squares.shape[1:])
            copies = []
            for k in range(1, n_fsdp):
                copy = remote(squares.at[0], squares.at[k], f_send.at[k], f_recv.at[k], f_dev(k))
                copy.start()
                copies.append(copy)
            for copy in copies:
                copy.wait()
            whole = squares[0]
            for k in range(1, n_fsdp):
                whole = whole + squares[k]
            factor = lax.rsqrt(whole[:, :1] / (depth * n_fsdp) + norm_eps)
            x[0, 0] = (mixed[...] * factor * gain[...]).astype(jnp.bfloat16)
            for copy in send_x():
                copy.wait()
        else:
            for k in range(n_fsdp):
                fin_out[k] = rows[k * 8 : (k + 1) * 8, :]
            copies = []
            for k in range(1, n_fsdp):
                there = lax.rem(f + k, n_fsdp)
                copy = remote(fin_out.at[there], fin_in.at[k], f_send.at[k], f_recv.at[k], f_dev(k))
                copy.start()
                copies.append(copy)
            out[f] = fin_out[f]
            for k in range(1, n_fsdp):
                copies[k - 1].wait()
                out[lax.rem(f - k + n_fsdp, n_fsdp)] = fin_in[k]


def shards(
    gate_up_master,
    gate_up_moment,
    gate_up_second,
    gate_up_grad,
    down_master,
    down_moment,
    down_second,
    down_grad,
    norm_gain,
    start_rows,
    queries,
    new_kv,
    kv_pool,
    page_table,
    cache_len,
):
    n_rep, n_fsdp, n_tp = (lax.axis_size(a) for a in ("rep", "fsdp", "tp"))
    n_group = n_rep * n_tp
    depth, cols = down_grad.shape
    local_rows, width = start_rows.shape
    steps = queries.shape[0]
    tiles = cols // TILE
    members = n_fsdp // 2
    block = local_rows * n_fsdp
    all_rows = block * n_group
    half = all_rows // 2

    attended = attend_all(queries, kv_pool, page_table, cache_len, new_kv)
    mixed = (start_rows.astype(jnp.float32) + attended[0]).astype(jnp.bfloat16).astype(jnp.float32)
    normed = mixed * lax.rsqrt(jnp.mean(mixed * mixed, axis=-1, keepdims=True) + norm_eps) * norm_gain
    pieces = jnp.concatenate([normed[None], mixed[None], attended[1:]], axis=0)
    pieces = pieces.reshape(steps + 1, local_rows, n_fsdp, depth).transpose(2, 0, 1, 3)
    pieces = pieces.reshape(n_fsdp, (steps + 1) * local_rows, depth)
    gain = lax.dynamic_index_in_dim(norm_gain.reshape(n_fsdp, 1, depth), lax.axis_index("fsdp"), 0, False)

    n_chunks = 3 * (depth // CHUNK)
    bf16, f32 = jnp.bfloat16, jnp.float32
    dma = pltpu.SemaphoreType.DMA
    final = pl.pallas_call(
        functools.partial(block_kernel, n_rep, n_fsdp, n_tp),
        out_shape=jax.ShapeDtypeStruct((n_fsdp, local_rows, depth), f32),
        in_specs=[pl.BlockSpec(memory_space=pl.ANY)] * 8 + [pl.BlockSpec(memory_space=pltpu.VMEM)] * 2,
        out_specs=pl.BlockSpec(memory_space=pltpu.VMEM),
        scratch_shapes=[
            pltpu.VMEM((3, depth, cols), bf16),
            pltpu.VMEM((SLOTS, 3, CHUNK, cols), f32),
            pltpu.VMEM((n_fsdp, (steps + 1) * local_rows, depth), f32),
            pltpu.VMEM((n_fsdp + n_group, 8, 128), f32),
            pltpu.VMEM((2, n_group // 2, block, depth), bf16),
            pltpu.VMEM((tiles, half, 2 * TILE), f32),
            pltpu.VMEM((tiles, half, 2 * TILE), bf16),
            pltpu.VMEM((tiles, half, 2 * TILE), bf16),
            pltpu.VMEM((tiles, members, half // members, 2 * TILE), bf16),
            pltpu.VMEM((tiles, members - 1, half // members, 2 * TILE), bf16),
            pltpu.VMEM((tiles, 2, members, half // members, TILE), bf16),
            pltpu.VMEM((all_rows, depth), f32),
            pltpu.VMEM((n_group, block, depth), bf16),
            pltpu.VMEM((n_group, block, depth), bf16),
            pltpu.VMEM((n_fsdp, block, 128), f32),
            pltpu.VMEM((block, depth), f32),
            pltpu.VMEM((n_fsdp, local_rows, depth), f32),
            pltpu.VMEM((n_fsdp, local_rows, depth), f32),
            dma((n_chunks,)),
            dma((SLOTS, 3)),
            dma((n_fsdp,)),
            dma((n_fsdp,)),
            dma((n_fsdp + n_group,)),
            dma((n_fsdp + n_group,)),
            dma((n_group,)),
            dma((n_group,)),
            dma((tiles,)),
            dma((tiles,)),
            dma((tiles, members - 1)),
            dma((tiles, members - 1)),
            dma((tiles, members - 1)),
            dma((tiles, members - 1)),
            dma((tiles,)),
            dma((tiles,)),
            dma((n_group,)),
            dma((n_group,)),
        ],
        compiler_params=pltpu.CompilerParams(
            collective_id=0, has_side_effects=True, vmem_limit_bytes=60 * 2**20
        ),
        cost_estimate=pl.CostEstimate(
            flops=2 * steps * all_rows * 3 * depth * cols,
            bytes_accessed=3 * depth * cols * 14,
            transcendentals=3 * depth * cols,
        ),
        name="update_and_decode",
    )(
        gate_up_master,
        gate_up_moment,
        gate_up_second,
        gate_up_grad,
        down_master,
        down_moment,
        down_second,
        down_grad,
        pieces,
        gain,
    )
    return final.transpose(1, 0, 2).reshape(local_rows, width).astype(jnp.bfloat16)


def solution(mesh):
    in_specs = (
        P(None, "fsdp", ("rep", "tp")),
        P(None, "fsdp", ("rep", "tp")),
        P(None, "fsdp", ("rep", "tp")),
        P(None, "fsdp", ("rep", "tp")),
        P("fsdp", ("rep", "tp")),
        P("fsdp", ("rep", "tp")),
        P("fsdp", ("rep", "tp")),
        P("fsdp", ("rep", "tp")),
        P(),
        P(("rep", "fsdp", "tp"), None),
        P(None, ("rep", "fsdp", "tp"), None),
        P(None, ("rep", "fsdp", "tp"), None, None),
        P(("rep", "fsdp", "tp"), None, None, None),
        P(("rep", "fsdp", "tp"), None),
        P(("rep", "fsdp", "tp")),
    )
    out_specs = P(("rep", "fsdp", "tp"), None)
    return jax.shard_map(shards, mesh=mesh, in_specs=in_specs, out_specs=out_specs, check_vma=False)
```

time: 840 us -> 150 us (0.18); the launches traced: 831 us -> 149 us
  waiting for transfers between devices: 457 us -> 0 us
  local copies, waits for them, and re-layouts: 208 us -> 13.8 us
  Pallas kernels: 0 us -> 125 us
  other arithmetic: 51.2 us -> 3.85 us
  blocking collectives: 42 us -> 0 us
  matrix products: 40.8 us -> 6.73 us
  between operations: 17.7 us -> 0.18 us
  starting transfers between devices: 13.7 us -> 0 us
    all_gather x4 -> x0, waiting for transfers between devices: 228 us -> none  [the longest x1 164 us: shards(): lax.all_gather(gate_up, 'rep', axis=2, tiled=True)]
    pallas_call x0 -> x1, Pallas kernels: none -> 125 us  [shards(): pl.pallas_call(functools.partial(block_kernel, n_rep, n_fsdp, n_tp), out_...]
    unnamed x29 -> x12, local copies, waits for them, and re-layouts: 119 us -> 0.03 us
    reduce_scatter x2 -> x0, waiting for transfers between devices: 117 us -> none  [shards(): lax.psum_scatter(lax.dot_general(hidden, roll_down, (((1,), (1,)), ((), (...]
    all_to_all x2 -> x0, waiting for transfers between devices: 112 us -> none  [the longest x1 112 us: shards(): lax.all_to_all(shaped[0], 'fsdp', split_axis=3, concat_axis=1, tiled=True)]
    psum x1 -> x0, blocking collectives: 42 us -> none  [shards(): total = lax.psum(local_squares, ('rep', 'fsdp', 'tp'))]
    convert_element_type x5 -> x2, other arithmetic: 37 us -> 1.63 us  [the longest x1 1.54 us: shards(): final.transpose(1, 0, 2).reshape(local_rows, width).astype(jnp.bfloat16)]
    dot_general x12 -> x4, matrix products: 40.8 us -> 6.73 us  [the longest x1 2.6 us: attend_all(): jnp.einsum('srjgh,cjh->jsrgc', query, keys, preferred_element_type=jnp.fl...]
  transfers between devices with their start and end apart: 8 -> 0, of which waited for: 6 -> 0; matrix products, arithmetic and copies ran while one was open for 24% -> 0% of each run, Pallas kernels for 0% -> 0%
where the time goes in v1:
time: 150 us; the launch traced here: 149 us
  Pallas kernels  125 us (83%)
  local copies, waits for them, and re-layouts  13.8 us (9%)
  matrix products  6.73 us (4%)
  other arithmetic  3.85 us (3%)
    pallas_call x1, Pallas kernels, shards(): pl.pallas_call(functools.partial(block_kernel, n_rep, n_fsdp, n_tp), out_...  125 us
    reshape x1, local copies, waits for them, and re-layouts, attend_all(): pool = kv_pool.reshape(pages * page, 2, heads, HD)  7.6 us
    slice x1, local copies, waits for them, and re-layouts, attend_all(): keys, values = (pool[:, 0], pool[:, 1])  4.5 us

profile of v1, /device:TPU:0, one launch (start us, length us, event | category | flops | bytes accessed | tf_op | source)
XLA Modules:
  0.0 149.5 jit_solution(4983422830867696438)
XLA Ops:
  0.0 7.6 %reshape.109 = bf16[1024,2,8,128]{3,2,1,0:T(8,128)(2,1)} reshape(bf16[64,16,2,1024]{3,2,1,0:T(2,128)(2,1)} %param.27) | data formatting | bytes 8388608 | tf_op jit(solution)/shard_map/reshape | solution.py:31
  7.6 0.0 copy-start.5
  7.6 0.0 copy-start.4
  7.6 0.0 copy-start
  7.6 4.5 %fusion.21 = (bf16[1024,1,8,128]{3,2,1,0:T(8,128)(2,1)}, bf16[1024,1,8,128]{3,2,1,0:T(8,128)(2,1)}) fusion(bf16[1024,2,8,128]{3,2,1,0:T(8,128)(2,1)} %reshape.109), kind=kLoop, calls=%fused_computation.44 | loop fusion | bytes 8388608 | tf_op jit(solution)/shard_map/slice | solution.py:32
  12.1 0.1 iota_add_fusion
  12.2 0.0 copy-done.5
  12.2 0.1 broadcast_compare_fusion
  12.3 0.0 copy-done.4
  12.3 0.1 iota_compare_fusion
  12.3 0.2 and_reduce_fusion
  12.6 0.2 copy.86
  12.7 0.2 broadcast_in_dim.26
  12.9 0.0 copy-done
  12.9 0.0 copy-start.2
  12.9 2.6 %fusion.2 = (f32[8,2,8,4]{2,3,1,0:T(4,128)S(1)}, f32[8,2,8,4,1024]{4,2,3,1,0:T(8,128)S(1)}) fusion(pred[8,1024]{1,0:T(8,128)(4,1)S(1)} %broadcast_in_dim.26, bf16[1024,1,8,128]{3,2,1,0:T(8,128)(2,1)} %get-tuple-element.7, bf16[2,8,8,4,128]{4,1,3,2,0:T(8,128)(2,1)S(1)} %bitcast.70), kind=kOutput, calls=%fused_computation.7 | convolution fusion | flops 135790080 | bytes 4335616 | tf_op jit(solution)/shard_map/srjgh,cjh->jsrgc/dot_general | solution.py:41
  15.6 0.0 copy-done.2
  15.6 1.3 fusion.12
  16.9 0.3 copy.93
  17.2 0.1 fusion.16
  17.3 0.1 fusion.15
  17.4 0.6 fusion.3
  18.0 0.1 divide_convert_fusion.2
  18.1 0.3 copy.104
  18.4 0.3 fusion.17
  18.7 0.0 copy-start.1
  18.7 0.0 copy-start.3
  18.7 2.6 %fusion.5 = f32[2,8,8,4,128]{4,1,3,0,2:T(8,128)S(1)} fusion(bf16[1024,1,8,128]{3,2,1,0:T(8,128)(2,1)} %get-tuple-element.8, f32[8,2,8,4,1024]{4,2,3,1,0:T(8,128)S(1)} %get-tuple-element.14, f32[8,2,8,4]{2,3,1,0:T(4,128)S(1)} %copy.101, f32[8,2,8,4]{2,3,1,0:T(4,128)S(1)} %copy.97, pred[8,1024]{1,0:T(8,128)(4,1)S(1)} %broadcast_in_dim.26, ...), kind=kOutput, calls=%fused_computation.10 | convolution fusion | flops 136904704 | bytes 4730880 | tf_op jit(solution)/shard_map/jsrgc,cjh->srjgh/dot_general | solution.py:52
  21.3 0.0 copy-done.1
  21.3 0.2 multiply_reduce_fusion
  21.5 0.0 copy-done.3
  21.5 0.1 multiply_multiply_fusion
  21.6 0.8 maximum_bitcast_fusion.pieces
  22.4 0.6 dynamic-slice_bitcast_fusion.gain
  23.0 125.0 %update_and_decode.1 = f32[4,8,1024]{2,1,0:T(8,128)} custom-call(f32[2,1024,1792]{2,1,0:T(8,128)} %gu_master.1, f32[2,1024,1792]{2,1,0:T(8,128)} %gu_moment.1, f32[2,1024,1792]{2,1,0:T(8,128)} %gu_second.1, bf16[2,1024,1792]{2,1,0:T(8,128)(2,1)} %gu_grad.1, f32[1024,1792]{1,0:T(8,128)} %d_master.1, f32[1024,1792]{1,0:T(8,128)} %d_moment.1, ...), custom_call_target="tpu_custom_call" | custom-call | flops 5637144576 | bytes 77070336 | tf_op jit(solution)/shard_map/update_and_decode/pallas_call | solution.py:457
  148.0 1.5 %convert_element_type.29 = bf16[4,8,1024]{2,1,0:T(8,128)(2,1)} convert(f32[4,8,1024]{2,1,0:T(8,128)} %update_and_decode.1) | non-fusion elementwise | flops 32768 | bytes 196608 | tf_op jit(solution)/shard_map/convert_element_type | solution.py:521
  (10 shorter events, 0.2 us)
Async XLA Ops:
  7.6 4.6 %copy-start.5 = (s32[8]{0:T(128)S(1)}, s32[8]{0:T(128)}, u32[]{:S(2)}) copy-start(s32[8]{0:T(128)} %param.29) | copy-start | bytes 100
  7.6 4.7 %copy-start.4 = (s32[8,8]{1,0:T(8,128)S(1)}, s32[8,8]{1,0:T(8,128)}, u32[]{:S(2)}) copy-start(s32[8,8]{1,0:T(8,128)} %param.28) | copy-start | bytes 772
  7.6 5.3 %copy-start = (bf16[2,8,4096]{2,1,0:T(8,128)(2,1)S(1)}, bf16[2,8,4096]{2,1,0:T(8,128)(2,1)}, u32[]{:S(2)}) copy-start(bf16[2,8,4096]{2,1,0:T(8,128)(2,1)} %param.25) | copy-start | bytes 393220
  12.9 2.6 %copy-start.2 = (bf16[2,8,2,1024]{3,2,1,0:T(2,128)(2,1)S(1)}, bf16[2,8,2,1024]{3,2,1,0:T(2,128)(2,1)}, u32[]{:S(2)}) copy-start(bf16[2,8,2,1024]{3,2,1,0:T(2,128)(2,1)} %param.26) | copy-start | bytes 196612
  18.7 2.7 %copy-start.1 = (bf16[8,4096]{1,0:T(8,128)(2,1)S(1)}, bf16[8,4096]{1,0:T(8,128)(2,1)}, u32[]{:S(2)}) copy-start(bf16[8,4096]{1,0:T(8,128)(2,1)} %param.24) | copy-start | bytes 196612
  18.7 2.8 %copy-start.3 = (f32[4096]{0:T(1024)S(1)}, f32[4096]{0:T(1024)}, u32[]{:S(2)}) copy-start(f32[4096]{0:T(1024)} %param.23) | copy-start | bytes 49156

commit v2 on v1

v2 whole, which is shorter than its diff:
```python
import functools

import jax
import jax.numpy as jnp
from jax import lax
from jax.experimental import pallas as pl
from jax.experimental.pallas import tpu as pltpu
from jax.sharding import PartitionSpec as P

HD = 128
FULL_WIDTH = 4096
MESH = pl.DeviceIdType.MESH

beta_one = 0.9
beta_two = 0.95
adam_eps = 1e-08
adam_time = 100.0
norm_eps = 1e-05

TILE = 256
SUB = 128
SLOTS = 4
LAG = 3


def split_inputs(kv_pool, page_table, cache_len, new_kv):
    rows, per_row = page_table.shape
    pages, page, _, kv_width = kv_pool.shape
    keys = kv_pool[:, :, 0, :].reshape(pages * page, kv_width)
    values = kv_pool[:, :, 1, :].reshape(pages * page, kv_width)
    place = (jnp.arange(per_row, dtype=jnp.int32) * page)[None, :, None, None] + jnp.arange(
        page, dtype=jnp.int32
    )
    named = page_table[:, :, None] == jnp.arange(pages, dtype=jnp.int32)
    valid = named[..., None] & (place < cache_len[:, None, None, None])
    valid = jnp.any(valid, axis=1).reshape(rows, pages * page).astype(jnp.float32)
    fresh = new_kv.astype(jnp.float32).transpose(0, 2, 1, 3)
    return keys, values, valid, fresh


def block_kernel(
    n_rep,
    n_fsdp,
    n_tp,
    gu_master,
    gu_moment,
    gu_second,
    gu_grad,
    d_master,
    d_moment,
    d_second,
    d_grad,
    gain,
    start,
    queries,
    keys,
    values,
    valid,
    fresh,
    out,
    weights,
    slots,
    att,
    pieces,
    got_pieces,
    att_out,
    att_in,
    sums,
    x,
    own,
    core_out,
    core_in,
    y_out,
    y_in,
    hid,
    acc,
    down_out,
    down_in,
    squares,
    mixed,
    fin_out,
    fin_in,
    grad_sem,
    slot_sem,
    f_send,
    f_recv,
    a_send,
    a_recv,
    s_send,
    s_recv,
    x_send,
    x_recv,
    core_send,
    core_recv,
    y_send,
    y_recv,
    h_send,
    h_recv,
    hc_send,
    hc_recv,
    d_send,
    d_recv,
):
    n_group = n_rep * n_tp
    members = n_fsdp // 2
    depth, cols = d_grad.shape
    tiles = cols // TILE
    steps = queries.shape[0]
    width = n_fsdp * depth
    units = 3 * tiles
    half = x.shape[1] * x.shape[2]
    part = half // members

    r = lax.axis_index("rep")
    f = lax.axis_index("fsdp")
    t = lax.axis_index("tp")
    g = r * n_tp + t
    c = lax.rem(f, 2)
    m = f // 2

    def f_dev(k):
        return (r, lax.rem(f + k, n_fsdp), t)

    def g_dev(k):
        there = lax.rem(g + k, n_group)
        return (there // n_tp, f, lax.rem(there, n_tp))

    def m_dev(k):
        return (r, lax.rem(m + k, members) * 2 + c, t)

    sibling = (r, m * 2 + 1 - c, t)

    barrier = pltpu.get_barrier_semaphore()
    for k in range(1, n_fsdp):
        pl.semaphore_signal(barrier, inc=1, device_id=f_dev(k), device_id_type=MESH)
    for k in range(1, n_group):
        pl.semaphore_signal(barrier, inc=1, device_id=g_dev(k), device_id_type=MESH)

    def tile_of(j):
        return pl.ds(pl.multiple_of(j * TILE, TILE), TILE)

    def grad_copies(j):
        at = tile_of(j)
        return [
            pltpu.make_async_copy(gu_grad.at[0, :, at], weights.at[0, j], grad_sem.at[0, j]),
            pltpu.make_async_copy(gu_grad.at[1, :, at], weights.at[1, j], grad_sem.at[1, j]),
            pltpu.make_async_copy(d_grad.at[:, at], weights.at[2, j], grad_sem.at[2, j]),
        ]

    def pair_copies(a, j):
        slot = lax.rem(2 * j + a, SLOTS)
        return [
            pltpu.make_async_copy(ref.at[a, :, tile_of(j)], slots.at[slot, i], slot_sem.at[slot, i])
            for i, ref in enumerate((gu_master, gu_moment, gu_second))
        ]

    def down_copies(j):
        slot = lax.rem(2 * tiles + j, SLOTS)
        return [
            pltpu.make_async_copy(ref.at[:, tile_of(j)], slots.at[slot, i], slot_sem.at[slot, i])
            for i, ref in enumerate((d_master, d_moment, d_second))
        ]

    def start_all(copies):
        for copy in copies:
            copy.start()

    def wait_all(copies):
        for copy in copies:
            copy.wait()

    def start_grads(j, carry):
        start_all(grad_copies(j))
        return carry

    lax.fori_loop(0, tiles, start_grads, 0)
    for n in range(SLOTS):
        start_all(pair_copies(n % 2, n // 2))

    pl.semaphore_wait(barrier, n_fsdp + n_group - 2)

    def remote(src, dst, send, recv, dev):
        return pltpu.make_async_remote_copy(
            src_ref=src, dst_ref=dst, send_sem=send, recv_sem=recv, device_id=dev, device_id_type=MESH
        )

    def squares_of(j, run):
        wait_all(grad_copies(j))
        for a in range(3):

            def square(b, run, a=a):
                v = weights[a, j, pl.ds(pl.multiple_of(b * SUB, SUB), SUB), :].astype(jnp.float32)
                return run + jnp.sum((v * v).reshape(SUB // 8, 8, TILE), axis=0)

            run = lax.fori_loop(0, depth // SUB, square, run)
        return run

    total = lax.fori_loop(0, tiles, squares_of, jnp.zeros((8, TILE), jnp.float32))
    tile_sum = total[:, :128]
    for b in range(1, TILE // 128):
        tile_sum = tile_sum + total[:, b * 128 : (b + 1) * 128]

    def send_sums(value, base, n, dev):
        sums[base] = value
        copies = [
            remote(sums.at[base], sums.at[base + k], s_send.at[base + k], s_recv.at[base + k], dev(k))
            for k in range(1, n)
        ]
        start_all(copies)
        return copies

    def add_sums(copies, value, base, n):
        wait_all(copies)
        for k in range(1, n):
            value = value + sums[base + k]
        return value

    def attend(step):
        heads = keys.shape[1] // HD
        group = width // keys.shape[1]
        scale = HD**-0.5
        mask = jnp.concatenate([valid[...]] * group, axis=0) > 0.5
        query = queries[step].astype(jnp.float32)
        for j in range(heads):
            lanes = slice(j * HD, (j + 1) * HD)
            q = jnp.concatenate(
                [query[:, (j * group + i) * HD : (j * group + i + 1) * HD] for i in range(group)], axis=0
            )
            old = lax.dot_general(
                q.astype(jnp.bfloat16),
                keys[:, lanes],
                (((1,), (1,)), ((), ())),
                preferred_element_type=jnp.float32,
            )
            old = jnp.where(mask, old * scale, -1e30)
            top = jnp.max(old, axis=1, keepdims=True)
            new = []
            for n in range(step + 1):
                k = jnp.concatenate([fresh[n, 0, :, lanes]] * group, axis=0)
                new.append(jnp.sum(q * k, axis=1, keepdims=True) * scale)
                top = jnp.maximum(top, new[n])
            old = jnp.exp(old - top)
            new = [jnp.exp(e - top) for e in new]
            whole = jnp.sum(old, axis=1, keepdims=True)
            for e in new:
                whole = whole + e
            y = jnp.dot(
                (old / whole).astype(jnp.bfloat16), values[:, lanes], preferred_element_type=jnp.float32
            )
            for n in range(step + 1):
                v = jnp.concatenate([fresh[n, 1, :, lanes]] * group, axis=0)
                y = y + (new[n] / whole).astype(jnp.bfloat16).astype(jnp.float32) * v
            for i in range(group):
                at = j * group + i
                att[:, at * HD : (at + 1) * HD] = y[i * 8 : (i + 1) * 8, :]

    sum_copies = send_sums(tile_sum, 0, n_fsdp, f_dev)
    attend(0)
    tile_sum = add_sums(sum_copies, tile_sum, 0, n_fsdp)
    sum_copies = send_sums(tile_sum, n_fsdp, n_group, g_dev)

    blend = (start[...].astype(jnp.float32) + att[...]).astype(jnp.bfloat16).astype(jnp.float32)
    factor = lax.rsqrt(jnp.sum(blend * blend, axis=1, keepdims=True) / width + norm_eps)
    for k in range(n_fsdp):
        cut = blend[:, k * depth : (k + 1) * depth]
        pieces[k, :8, :] = cut * factor * gain[k]
        pieces[k, 8:, :] = cut
    piece_copies = []
    for k in range(1, n_fsdp):
        there = lax.rem(f + k, n_fsdp)
        piece_copies.append(
            remote(pieces.at[there], got_pieces.at[k], f_send.at[k], f_recv.at[k], f_dev(k))
        )
    start_all(piece_copies)
    got_pieces[0] = pieces[f]
    wait_all(piece_copies)

    def joined(ref, a):
        at = pl.ds(a * 8, 8)
        blocks = [ref[lax.rem(f - b + n_fsdp, n_fsdp), at, :] for b in range(n_fsdp)]
        return jnp.concatenate(blocks, axis=0)

    x[0, 0] = joined(got_pieces, 0).astype(jnp.bfloat16)
    mixed[...] = joined(got_pieces, 1)

    def x_copies():
        return [
            remote(
                x.at[0, 0], x.at[k // x.shape[1], k % x.shape[1]], x_send.at[k], x_recv.at[k], g_dev(k)
            )
            for k in range(1, n_group)
        ]

    start_all(x_copies())
    tile_sum = add_sums(sum_copies, tile_sum, n_fsdp, n_group)
    clip = jnp.minimum(1.0, lax.rsqrt(jnp.sum(tile_sum, keepdims=True)))

    rate = 2.0 / FULL_WIDTH**0.5 / (1.0 - beta_one**adam_time)
    keep_m = rate * beta_one
    add_m = rate * (1.0 - beta_one)
    second_fix = 1.0 - beta_two**adam_time
    keep_v = beta_two / second_fix
    add_v = (1.0 - beta_two) / second_fix

    def update(s, j, slot):
        def rows_at(b, carry):
            at = pl.ds(pl.multiple_of(b * SUB, SUB), SUB)
            grad = weights[s, j, at, :].astype(jnp.float32) * clip
            first = keep_m * slots[slot, 1, at, :] + add_m * grad
            second = keep_v * slots[slot, 2, at, :] + add_v * (grad * grad)
            new = slots[slot, 0, at, :] - first / (jnp.sqrt(second) + adam_eps)
            weights[s, j, at, :] = new.astype(jnp.bfloat16)
            return carry

        lax.fori_loop(0, depth // SUB, rows_at, 0)


    def core_copy(j):
        return remote(core_out.at[j], core_in.at[j], core_send.at[j], core_recv.at[j], sibling)

    def y_copy(j, k):
        there = lax.rem(m + k, members)
        return remote(
            y_out.at[j, there], y_in.at[j, k - 1], y_send.at[j, k - 1], y_recv.at[j, k - 1], m_dev(k)
        )

    def h_copy(j, k):
        return remote(
            hid.at[j, c, m], hid.at[j, c, m], h_send.at[j, k - 1], h_recv.at[j, k - 1], m_dev(k)
        )

    def h_arrival(j, k):
        there = lax.rem(m - k + members, members)
        return remote(
            hid.at[j, c, m], hid.at[j, c, there], h_send.at[j, k - 1], h_recv.at[j, k - 1], m_dev(k)
        )

    def hc_copy(j):
        return remote(hid.at[j, c], hid.at[j, c], hc_send.at[j], hc_recv.at[j], sibling)

    def hc_arrival(j):
        return remote(hid.at[j, c], hid.at[j, 1 - c], hc_send.at[j], hc_recv.at[j], sibling)

    def multiply(j):
        theirs = x[1 - c].reshape(half, depth)
        mine = x[c].reshape(half, depth)
        both = jnp.concatenate([theirs, mine], axis=0)
        for a in range(2):
            y = jnp.dot(both, weights[a, j], preferred_element_type=jnp.float32)
            core_out[j, :, a * TILE : (a + 1) * TILE] = y[:half].astype(jnp.bfloat16)
            own[j, :, a * TILE : (a + 1) * TILE] = y[half:]
        core_copy(j).start()

    def add_core(j):
        core_copy(j).wait()
        y = own[j] + core_in[j].astype(jnp.float32)
        own[j] = y
        y_out[j] = y.astype(jnp.bfloat16).reshape(members, part, 2 * TILE)
        for k in range(1, members):
            y_copy(j, k).start()

    def second_stage(j):
        y = own[j, pl.ds(pl.multiple_of(m * part, part), part), :]
        for k in range(1, members):
            y_copy(j, k).wait()
            y = y + y_in[j, k - 1].astype(jnp.float32)
        gate, upper = y[:, :TILE], y[:, TILE:]
        hid[j, c, m] = (gate * jax.nn.sigmoid(gate) * upper).astype(jnp.bfloat16)
        for k in range(1, members):
            h_copy(j, k).start()

    def third_stage(j):
        for k in range(1, members):
            h_copy(j, k).wait_send()
            h_arrival(j, k).wait_recv()
        hc_copy(j).start()

    def fourth_stage(j):
        hc_copy(j).wait_send()
        hc_arrival(j).wait_recv()
        acc[...] += lax.dot_general(
            hid[j].reshape(2 * half, TILE),
            weights[2, j],
            (((1,), (1,)), ((), ())),
            preferred_element_type=jnp.float32,
        )

    def after(j, first, stage):
        @pl.when(first <= j)
        def _():
            stage(j - first)

    def before(j, first, stage):
        @pl.when(j < tiles - first)
        def _():
            stage(j + first)

    def update_pair(j, carry):
        for a in range(2):
            wait_all(pair_copies(a, j))
            update(a, j, lax.rem(2 * j + a, SLOTS))

            @pl.when(j + SLOTS // 2 < tiles)
            def _():
                start_all(pair_copies(a, j + SLOTS // 2))

            @pl.when(j + SLOTS // 2 >= tiles)
            def _():
                start_all(down_copies(2 * (j + SLOTS // 2 - tiles) + a))

        @pl.when(j == LAG)
        def _():
            wait_all(x_copies())

        after(j, LAG, multiply)
        after(j, LAG + 1, add_core)
        after(j, LAG + 2, second_stage)
        after(j, LAG + 3, third_stage)
        return carry

    def update_down(j, carry):
        wait_all(down_copies(j))
        update(2, j, lax.rem(2 * tiles + j, SLOTS))

        @pl.when(j + SLOTS < tiles)
        def _():
            start_all(down_copies(j + SLOTS))

        before(j, tiles - LAG, multiply)
        before(j, tiles - LAG - 1, add_core)
        before(j, tiles - LAG - 2, second_stage)
        before(j, tiles - LAG - 3, third_stage)
        after(j, 2, fourth_stage)
        return carry

    def looped(stage, first, last):
        def body(j, carry):
            stage(j)
            return carry

        lax.fori_loop(first, last, body, 0)

    for step in range(steps):
        acc[...] = jnp.zeros_like(acc)
        if step == 0:
            lax.fori_loop(0, tiles, update_pair, 0)
            lax.fori_loop(0, tiles, update_down, 0)
            looped(fourth_stage, tiles - 2, tiles)
        else:

            def first_stage(j):
                multiply(j)
                after(j, 1, add_core)

            looped(first_stage, 0, tiles)
            add_core(tiles - 1)
            looped(second_stage, 0, tiles)
            looped(third_stage, 0, tiles)
            looped(fourth_stage, 0, tiles)

        rows_of = acc.shape[0] // n_group
        copies = []
        for k in range(1, n_group):
            down_out[k] = acc[k * rows_of : (k + 1) * rows_of, :].astype(jnp.bfloat16)
            copy = remote(
                down_out.at[k], down_in.at[k], d_send.at[k], d_recv.at[k], g_dev(n_group - k)
            )
            copy.start()
            copies.append(copy)
        if step < steps - 1:
            attend(step + 1)
            for k in range(n_fsdp):
                att_out[k] = att[:, k * depth : (k + 1) * depth]
            att_copies = [
                remote(
                    att_out.at[lax.rem(f + k, n_fsdp)], att_in.at[k], a_send.at[k], a_recv.at[k], f_dev(k)
                )
                for k in range(1, n_fsdp)
            ]
            start_all(att_copies)
            att_in[0] = att_out[f]
            wait_all(att_copies)
        summed = acc[:rows_of, :]
        for k in range(1, n_group):
            copies[k - 1].wait()
            summed = summed + down_in[k].astype(jnp.float32)
        rows = (mixed[...] + summed).astype(jnp.bfloat16).astype(jnp.float32)

        if step < steps - 1:
            blend = (rows + joined(att_in, 0)).astype(jnp.bfloat16).astype(jnp.float32)
            mixed[...] = blend
            local = jnp.sum(blend * blend, axis=1, keepdims=True)
            squares[0] = jnp.broadcast_to(local, squares.shape[1:])
            copies = []
            for k in range(1, n_fsdp):
                copy = remote(squares.at[0], squares.at[k], f_send.at[k], f_recv.at[k], f_dev(k))
                copy.start()
                copies.append(copy)
            for copy in copies:
                copy.wait()
            whole = squares[0]
            for k in range(1, n_fsdp):
                whole = whole + squares[k]
            factor = lax.rsqrt(whole[:, :1] / (depth * n_fsdp) + norm_eps)
            x[0, 0] = (mixed[...] * factor * gain[f]).astype(jnp.bfloat16)
            start_all(x_copies())
            wait_all(x_copies())
        else:
            for k in range(n_fsdp):
                fin_out[k] = rows[k * 8 : (k + 1) * 8, :]
            copies = []
            for k in range(1, n_fsdp):
                there = lax.rem(f + k, n_fsdp)
                copy = remote(fin_out.at[there], fin_in.at[k], f_send.at[k], f_recv.at[k], f_dev(k))
                copy.start()
                copies.append(copy)
            out[f] = fin_out[f]
            for k in range(1, n_fsdp):
                copies[k - 1].wait()
                out[lax.rem(f - k + n_fsdp, n_fsdp)] = fin_in[k]


def shards(
    gate_up_master,
    gate_up_moment,
    gate_up_second,
    gate_up_grad,
    down_master,
    down_moment,
    down_second,
    down_grad,
    norm_gain,
    start_rows,
    queries,
    new_kv,
    kv_pool,
    page_table,
    cache_len,
):
    n_rep, n_fsdp, n_tp = (lax.axis_size(a) for a in ("rep", "fsdp", "tp"))
    n_group = n_rep * n_tp
    depth, cols = down_grad.shape
    local_rows, width = start_rows.shape
    steps = queries.shape[0]
    tiles = cols // TILE
    members = n_fsdp // 2
    block = local_rows * n_fsdp
    all_rows = block * n_group
    half = all_rows // 2

    keys, values, valid, fresh = split_inputs(kv_pool, page_table, cache_len, new_kv)
    gain = norm_gain.reshape(n_fsdp, 1, depth)

    bf16, f32 = jnp.bfloat16, jnp.float32
    dma = pltpu.SemaphoreType.DMA
    final = pl.pallas_call(
        functools.partial(block_kernel, n_rep, n_fsdp, n_tp),
        out_shape=jax.ShapeDtypeStruct((n_fsdp, local_rows, depth), f32),
        in_specs=[pl.BlockSpec(memory_space=pl.ANY)] * 8 + [pl.BlockSpec(memory_space=pltpu.VMEM)] * 7,
        out_specs=pl.BlockSpec(memory_space=pltpu.VMEM),
        scratch_shapes=[
            pltpu.VMEM((3, tiles, depth, TILE), bf16),
            pltpu.VMEM((SLOTS, 3, depth, TILE), f32),
            pltpu.VMEM((local_rows, width), f32),
            pltpu.VMEM((n_fsdp, 2 * local_rows, depth), f32),
            pltpu.VMEM((n_fsdp, 2 * local_rows, depth), f32),
            pltpu.VMEM((n_fsdp, local_rows, depth), f32),
            pltpu.VMEM((n_fsdp, local_rows, depth), f32),
            pltpu.VMEM((n_fsdp + n_group, 8, 128), f32),
            pltpu.VMEM((2, n_group // 2, block, depth), bf16),
            pltpu.VMEM((tiles, half, 2 * TILE), f32),
            pltpu.VMEM((tiles, half, 2 * TILE), bf16),
            pltpu.VMEM((tiles, half, 2 * TILE), bf16),
            pltpu.VMEM((tiles, members, half // members, 2 * TILE), bf16),
            pltpu.VMEM((tiles, members - 1, half // members, 2 * TILE), bf16),
            pltpu.VMEM((tiles, 2, members, half // members, TILE), bf16),
            pltpu.VMEM((all_rows, depth), f32),
            pltpu.VMEM((n_group, block, depth), bf16),
            pltpu.VMEM((n_group, block, depth), bf16),
            pltpu.VMEM((n_fsdp, block, 128), f32),
            pltpu.VMEM((block, depth), f32),
            pltpu.VMEM((n_fsdp, local_rows, depth), f32),
            pltpu.VMEM((n_fsdp, local_rows, depth), f32),
            dma((3, tiles)),
            dma((SLOTS, 3)),
            dma((n_fsdp,)),
            dma((n_fsdp,)),
            dma((n_fsdp,)),
            dma((n_fsdp,)),
            dma((n_fsdp + n_group,)),
            dma((n_fsdp + n_group,)),
            dma((n_group,)),
            dma((n_group,)),
            dma((tiles,)),
            dma((tiles,)),
            dma((tiles, members - 1)),
            dma((tiles, members - 1)),
            dma((tiles, members - 1)),
            dma((tiles, members - 1)),
            dma((tiles,)),
            dma((tiles,)),
            dma((n_group,)),
            dma((n_group,)),
        ],
        compiler_params=pltpu.CompilerParams(
            collective_id=0, has_side_effects=True, vmem_limit_bytes=60 * 2**20
        ),
        cost_estimate=pl.CostEstimate(
            flops=2 * steps * all_rows * 3 * depth * cols,
            bytes_accessed=3 * depth * cols * 14,
            transcendentals=3 * depth * cols,
        ),
        name="update_and_decode",
    )(
        gate_up_master,
        gate_up_moment,
        gate_up_second,
        gate_up_grad,
        down_master,
        down_moment,
        down_second,
        down_grad,
        gain,
        start_rows,
        queries,
        keys,
        values,
        valid,
        fresh,
    )
    return final.transpose(1, 0, 2).reshape(local_rows, width).astype(jnp.bfloat16)


def solution(mesh):
    in_specs = (
        P(None, "fsdp", ("rep", "tp")),
        P(None, "fsdp", ("rep", "tp")),
        P(None, "fsdp", ("rep", "tp")),
        P(None, "fsdp", ("rep", "tp")),
        P("fsdp", ("rep", "tp")),
        P("fsdp", ("rep", "tp")),
        P("fsdp", ("rep", "tp")),
        P("fsdp", ("rep", "tp")),
        P(),
        P(("rep", "fsdp", "tp"), None),
        P(None, ("rep", "fsdp", "tp"), None),
        P(None, ("rep", "fsdp", "tp"), None, None),
        P(("rep", "fsdp", "tp"), None, None, None),
        P(("rep", "fsdp", "tp"), None),
        P(("rep", "fsdp", "tp")),
    )
    out_specs = P(("rep", "fsdp", "tp"), None)
    return jax.shard_map(shards, mesh=mesh, in_specs=in_specs, out_specs=out_specs, check_vma=False)
```

time: 150 us -> 143 us (0.953)
  matrix products: 6.73 us -> 0 us
  local copies, waits for them, and re-layouts: 13.8 us -> 15.4 us
    reshape x2 -> x0, local copies, waits for them, and re-layouts: 7.65 us -> none  [the longest x1 7.6 us: attend_all(): pool = kv_pool.reshape(pages * page, 2, heads, HD)]
    dot_general x4 -> x0, matrix products: 6.73 us -> none  [the longest x1 2.6 us: attend_all(): jnp.einsum('srjgh,cjh->jsrgc', query, keys, preferred_element_type=jnp.fl...]
    slice x3 -> x1, local copies, waits for them, and re-layouts: 4.53 us -> 10.2 us  [split_inputs(): values = kv_pool[:, :, 1, :].reshape(pages * page, kv_width)]
    unnamed x12 -> x8, local copies, waits for them, and re-layouts: 0.03 us -> 4.27 us
where the time goes in v2:
time: 143 us
  Pallas kernels  125 us (87%)
  local copies, waits for them, and re-layouts  15.4 us (11%)
  other arithmetic  2.64 us (2%)
    pallas_call x1, Pallas kernels, shards(): pl.pallas_call(functools.partial(block_kernel, n_rep, n_fsdp, n_tp), out_...  125 us
    slice x1, local copies, waits for them, and re-layouts, split_inputs(): values = kv_pool[:, :, 1, :].reshape(pages * page, kv_width)  10.2 us
    unnamed x8, local copies, waits for them, and re-layouts  4.27 us

profile of v2, /device:TPU:0, one launch (start us, length us, event | category | flops | bytes accessed | tf_op | source)
XLA Modules:
  0.0 143.2 jit_solution(15814536294885648130)
XLA Ops:
  0.0 10.2 %fusion = (bf16[64,16,1,1024]{3,2,1,0:T(2,128)(2,1)S(1)}, bf16[64,16,1,1024]{3,2,1,0:T(2,128)(2,1)S(1)}) fusion(bf16[64,16,2,1024]{3,2,1,0:T(2,128)(2,1)} %param.27), kind=kLoop, calls=%fused_computation.6 | loop fusion | bytes 8388608 | tf_op jit(solution)/shard_map/slice | solution.py:30
  10.2 2.2 %copy.24 = bf16[64,16,1,1024]{3,1,0,2:T(8,128)(2,1)} copy(bf16[64,16,1,1024]{3,2,1,0:T(2,128)(2,1)S(1)} %get-tuple-element.6) | data formatting | bytes 4194304
  12.4 0.0 copy-start.2
  12.4 0.0 copy-start.1
  12.4 0.0 copy-start
  12.4 2.1 %copy.25 = bf16[64,16,1,1024]{3,1,0,2:T(8,128)(2,1)} copy(bf16[64,16,1,1024]{3,2,1,0:T(2,128)(2,1)S(1)} %get-tuple-element.5) | data formatting | bytes 4194304
  14.5 0.1 iota_add_fusion
  14.5 0.0 copy-done.2
  14.6 0.1 broadcast_compare_fusion
  14.6 0.0 copy-done.1
  14.6 0.1 iota_compare_fusion
  14.7 0.2 and_reduce_fusion
  14.9 0.1 copy.22
  15.1 0.8 reshape.47.valid
  15.8 0.0 copy-done
  15.8 0.7 convert_bitcast_fusion.fresh
  16.5 125.1 %update_and_decode.1 = f32[4,8,1024]{2,1,0:T(8,128)} custom-call(f32[2,1024,1792]{2,1,0:T(8,128)} %gu_master.1, f32[2,1024,1792]{2,1,0:T(8,128)} %gu_moment.1, f32[2,1024,1792]{2,1,0:T(8,128)} %gu_second.1, bf16[2,1024,1792]{2,1,0:T(8,128)(2,1)} %gu_grad.1, f32[1024,1792]{1,0:T(8,128)} %d_master.1, f32[1024,1792]{1,0:T(8,128)} %d_moment.1, ...), custom_call_target="tpu_custom_call" | custom-call | flops 5637144576 | bytes 77070336 | tf_op jit(solution)/shard_map/update_and_decode/pallas_call | solution.py:556
  141.6 1.5 %convert_element_type.17 = bf16[4,8,1024]{2,1,0:T(8,128)(2,1)} convert(f32[4,8,1024]{2,1,0:T(8,128)} %update_and_decode.1) | non-fusion elementwise | flops 32768 | bytes 196608 | tf_op jit(solution)/shard_map/convert_element_type | solution.py:631
  (2 shorter events, 0.0 us)
Async XLA Ops:
  12.4 2.2 %copy-start.2 = (s32[8]{0:T(128)S(1)}, s32[8]{0:T(128)}, u32[]{:S(2)}) copy-start(s32[8]{0:T(128)} %param.29) | copy-start | bytes 100
  12.4 2.3 %copy-start.1 = (s32[8,8]{1,0:T(8,128)S(1)}, s32[8,8]{1,0:T(8,128)}, u32[]{:S(2)}) copy-start(s32[8,8]{1,0:T(8,128)} %param.28) | copy-start | bytes 772
  12.4 3.5 %copy-start = (bf16[2,8,2,1024]{3,2,1,0:T(2,128)(2,1)S(1)}, bf16[2,8,2,1024]{3,2,1,0:T(2,128)(2,1)}, u32[]{:S(2)}) copy-start(bf16[2,8,2,1024]{3,2,1,0:T(2,128)(2,1)} %param.26) | copy-start | bytes 196612

commit v3 on v2

--- a/solution.py
+++ b/solution.py
@@ -18,30 +18,17 @@
 norm_eps = 1e-05
 
 TILE = 256
-SUB = 128
+SUB = 32
+SQUARES = 128
 SLOTS = 4
 LAG = 3
-
-
-def split_inputs(kv_pool, page_table, cache_len, new_kv):
-    rows, per_row = page_table.shape
-    pages, page, _, kv_width = kv_pool.shape
-    keys = kv_pool[:, :, 0, :].reshape(pages * page, kv_width)
-    values = kv_pool[:, :, 1, :].reshape(pages * page, kv_width)
-    place = (jnp.arange(per_row, dtype=jnp.int32) * page)[None, :, None, None] + jnp.arange(
-        page, dtype=jnp.int32
-    )
-    named = page_table[:, :, None] == jnp.arange(pages, dtype=jnp.int32)
-    valid = named[..., None] & (place < cache_len[:, None, None, None])
-    valid = jnp.any(valid, axis=1).reshape(rows, pages * page).astype(jnp.float32)
-    fresh = new_kv.astype(jnp.float32).transpose(0, 2, 1, 3)
-    return keys, values, valid, fresh
 
 
 def block_kernel(
     n_rep,
     n_fsdp,
     n_tp,
+    page,
     gu_master,
     gu_moment,
     gu_second,
@@ -53,13 +40,15 @@
     gain,
     start,
     queries,
-    keys,
-    values,
-    valid,
+    kv_raw,
+    table,
+    length,
     fresh,
     out,
     weights,
     slots,
+    kv,
+    valid,
     att,
     pieces,
     got_pieces,
@@ -125,6 +114,12 @@
         there = lax.rem(g + k, n_group)
         return (there // n_tp, f, lax.rem(there, n_tp))
 
+    def z_dev(k):
+        return (r, f, lax.rem(t + k, n_tp))
+
+    def r_dev(k):
+        return (lax.rem(r + k, n_rep), f, t)
+
     def m_dev(k):
         return (r, lax.rem(m + k, members) * 2 + c, t)
 
@@ -189,10 +184,11 @@
         for a in range(3):
 
             def square(b, run, a=a):
-                v = weights[a, j, pl.ds(pl.multiple_of(b * SUB, SUB), SUB), :].astype(jnp.float32)
-                return run + jnp.sum((v * v).reshape(SUB // 8, 8, TILE), axis=0)
-
-            run = lax.fori_loop(0, depth // SUB, square, run)
+                v = weights[a, j, pl.ds(pl.multiple_of(b * SQUARES, SQUARES), SQUARES), :]
+                v = v.astype(jnp.float32)
+                return run + jnp.sum((v * v).reshape(SQUARES // 8, 8, TILE), axis=0)
+
+            run = lax.fori_loop(0, depth // SQUARES, square, run)
         return run
 
     total = lax.fori_loop(0, tiles, squares_of, jnp.zeros((8, TILE), jnp.float32))
@@ -215,22 +211,35 @@
             value = value + sums[base + k]
         return value
 
-    def attend(step):
-        heads = keys.shape[1] // HD
-        group = width // keys.shape[1]
+    def unpage(b, carry):
+        at = pl.ds(pl.multiple_of(b * 2 * page, 2 * page), 2 * page)
+        kv[at, :] = kv_raw[b].reshape(2 * page, kv.shape[1])
+        return carry
+
+    lax.fori_loop(0, kv_raw.shape[0], unpage, 0)
+
+    lane = lax.broadcasted_iota(jnp.int32, valid.shape, 1)
+    place = lax.rem(lane // 2, page)
+    held = jnp.zeros(valid.shape, jnp.float32)
+    for p in range(table.shape[1]):
+        named = table[:, p : p + 1] == lane // (2 * page)
+        held = jnp.where(named & (place + p * page < length[...]), 1.0, held)
+    valid[...] = jnp.where(lax.rem(lane, 2) == 0, held, 0.0)
+
+    heads = kv.shape[1] // HD
+    group = width // kv.shape[1]
+
+    def attend(step, first, last):
         scale = HD**-0.5
         mask = jnp.concatenate([valid[...]] * group, axis=0) > 0.5
         query = queries[step].astype(jnp.float32)
-        for j in range(heads):
+        for j in range(first, last):
             lanes = slice(j * HD, (j + 1) * HD)
             q = jnp.concatenate(
                 [query[:, (j * group + i) * HD : (j * group + i + 1) * HD] for i in range(group)], axis=0
             )
             old = lax.dot_general(
-                q.astype(jnp.bfloat16),
-                keys[:, lanes],
-                (((1,), (1,)), ((), ())),
-                preferred_element_type=jnp.float32,
+                q.astype(jnp.bfloat16), kv[:, lanes], (((1,), (1,)), ((), ())), preferred_element_type=jnp.float32
             )
             old = jnp.where(mask, old * scale, -1e30)
             top = jnp.max(old, axis=1, keepdims=True)
@@ -244,18 +253,18 @@
             whole = jnp.sum(old, axis=1, keepdims=True)
             for e in new:
                 whole = whole + e
-            y = jnp.dot(
-                (old / whole).astype(jnp.bfloat16), values[:, lanes], preferred_element_type=jnp.float32
-            )
+            inverse = 1.0 / whole
+            prob = pltpu.roll(old * inverse, 1, 1).astype(jnp.bfloat16)
+            y = jnp.dot(prob, kv[:, lanes], preferred_element_type=jnp.float32)
             for n in range(step + 1):
                 v = jnp.concatenate([fresh[n, 1, :, lanes]] * group, axis=0)
-                y = y + (new[n] / whole).astype(jnp.bfloat16).astype(jnp.float32) * v
+                y = y + (new[n] * inverse).astype(jnp.bfloat16).astype(jnp.float32) * v
             for i in range(group):
                 at = j * group + i
                 att[:, at * HD : (at + 1) * HD] = y[i * 8 : (i + 1) * 8, :]
 
     sum_copies = send_sums(tile_sum, 0, n_fsdp, f_dev)
-    attend(0)
+    attend(0, 0, heads)
     tile_sum = add_sums(sum_copies, tile_sum, 0, n_fsdp)
     sum_copies = send_sums(tile_sum, n_fsdp, n_group, g_dev)
 
@@ -283,15 +292,34 @@
     x[0, 0] = joined(got_pieces, 0).astype(jnp.bfloat16)
     mixed[...] = joined(got_pieces, 1)
 
-    def x_copies():
+    def x_block(i):
+        return x.at[i // x.shape[1], i % x.shape[1]]
+
+    def x_along_tp():
         return [
-            remote(
-                x.at[0, 0], x.at[k // x.shape[1], k % x.shape[1]], x_send.at[k], x_recv.at[k], g_dev(k)
-            )
-            for k in range(1, n_group)
+            remote(x_block(0), x_block(k), x_send.at[k], x_recv.at[k], z_dev(k)) for k in range(1, n_tp)
         ]
 
-    start_all(x_copies())
+    def x_along_rep(k):
+        return [
+            remote(x_block(k), x_block(i * n_tp + k), x_send.at[i * n_tp + k], x_recv.at[i * n_tp + k], r_dev(i))
+            for i in range(1, n_rep)
+        ]
+
+    def x_start():
+        start_all(x_along_tp())
+        start_all(x_along_rep(0))
+
+    def x_forward():
+        for k, copy in enumerate(x_along_tp(), 1):
+            copy.wait()
+            start_all(x_along_rep(k))
+
+    def x_finish():
+        for k in range(n_tp):
+            wait_all(x_along_rep(k))
+
+    x_start()
     tile_sum = add_sums(sum_copies, tile_sum, n_fsdp, n_group)
     clip = jnp.minimum(1.0, lax.rsqrt(jnp.sum(tile_sum, keepdims=True)))
 
@@ -302,17 +330,23 @@
     keep_v = beta_two / second_fix
     add_v = (1.0 - beta_two) / second_fix
 
+    clip_m = add_m * clip
+    clip_v = add_v * clip * clip
+
     def update(s, j, slot):
         def rows_at(b, carry):
             at = pl.ds(pl.multiple_of(b * SUB, SUB), SUB)
-            grad = weights[s, j, at, :].astype(jnp.float32) * clip
-            first = keep_m * slots[slot, 1, at, :] + add_m * grad
-            second = keep_v * slots[slot, 2, at, :] + add_v * (grad * grad)
-            new = slots[slot, 0, at, :] - first / (jnp.sqrt(second) + adam_eps)
+            grad = weights[s, j, at, :].astype(jnp.float32)
+            first = keep_m * slots[slot, 1, at, :] + clip_m * grad
+            second = keep_v * slots[slot, 2, at, :] + clip_v * (grad * grad)
+            under = second * lax.rsqrt(second) + adam_eps
+            inverse = pl.reciprocal(under, approx=True)
+            inverse = inverse * (2.0 - under * inverse)
+            new = slots[slot, 0, at, :] - first * inverse
             weights[s, j, at, :] = new.astype(jnp.bfloat16)
             return carry
 
-        lax.fori_loop(0, depth // SUB, rows_at, 0)
+        lax.fori_loop(0, depth // SUB, rows_at, 0, unroll=2)
 
 
     def core_copy(j):
@@ -408,9 +442,13 @@
             def _():
                 start_all(down_copies(2 * (j + SLOTS // 2 - tiles) + a))
 
+        @pl.when(j == LAG - 2)
+        def _():
+            x_forward()
+
         @pl.when(j == LAG)
         def _():
-            wait_all(x_copies())
+            x_finish()
 
         after(j, LAG, multiply)
         after(j, LAG + 1, add_core)
@@ -459,16 +497,38 @@
             looped(fourth_stage, 0, tiles)
 
         rows_of = acc.shape[0] // n_group
-        copies = []
-        for k in range(1, n_group):
-            down_out[k] = acc[k * rows_of : (k + 1) * rows_of, :].astype(jnp.bfloat16)
-            copy = remote(
-                down_out.at[k], down_in.at[k], d_send.at[k], d_recv.at[k], g_dev(n_group - k)
-            )
-            copy.start()
-            copies.append(copy)
+
+        def own_block(i):
+            return acc[i * rows_of : (i + 1) * rows_of, :]
+
+        def down_along_rep(k):
+            return [
+                remote(down_out.at[i], down_in.at[i], d_send.at[i], d_recv.at[i], r_dev(n_rep - i // n_tp))
+                for i in range(n_tp + k, n_group, n_tp)
+            ]
+
+        def down_along_tp(k):
+            return remote(down_out.at[k], down_in.at[k], d_send.at[k], d_recv.at[k], z_dev(n_tp - k))
+
+        order = list(range(1, n_tp)) + [0]
+        for k in order:
+            for i in range(n_tp + k, n_group, n_tp):
+                down_out[i] = own_block(i).astype(jnp.bfloat16)
+            start_all(down_along_rep(k))
+        summed = None
+        done = 0
+        for n, k in enumerate(order):
+            if step < steps - 1:
+                attend(step + 1, done, heads * (n + 1) // n_tp)
+                done = heads * (n + 1) // n_tp
+            wait_all(down_along_rep(k))
+            summed = own_block(k)
+            for i in range(n_tp + k, n_group, n_tp):
+                summed = summed + down_in[i].astype(jnp.float32)
+            if k > 0:
+                down_out[k] = summed.astype(jnp.bfloat16)
+                down_along_tp(k).start()
         if step < steps - 1:
-            attend(step + 1)
             for k in range(n_fsdp):
                 att_out[k] = att[:, k * depth : (k + 1) * depth]
             att_copies = [
@@ -480,9 +540,8 @@
             start_all(att_copies)
             att_in[0] = att_out[f]
             wait_all(att_copies)
-        summed = acc[:rows_of, :]
-        for k in range(1, n_group):
-            copies[k - 1].wait()
+        for k in range(1, n_tp):
+            down_along_tp(k).wait()
             summed = summed + down_in[k].astype(jnp.float32)
         rows = (mixed[...] + summed).astype(jnp.bfloat16).astype(jnp.float32)
 
@@ -503,8 +562,9 @@
                 whole = whole + squares[k]
             factor = lax.rsqrt(whole[:, :1] / (depth * n_fsdp) + norm_eps)
             x[0, 0] = (mixed[...] * factor * gain[f]).astype(jnp.bfloat16)
-            start_all(x_copies())
-            wait_all(x_copies())
+            x_start()
+            x_forward()
+            x_finish()
         else:
             for k in range(n_fsdp):
                 fin_out[k] = rows[k * 8 : (k + 1) * 8, :]
@@ -548,19 +608,23 @@
     all_rows = block * n_group
     half = all_rows // 2
 
-    keys, values, valid, fresh = split_inputs(kv_pool, page_table, cache_len, new_kv)
+    pages, page, _, kv_width = kv_pool.shape
+    kv = kv_pool
+    fresh = new_kv.astype(jnp.float32).transpose(0, 2, 1, 3)
     gain = norm_gain.reshape(n_fsdp, 1, depth)
 
     bf16, f32 = jnp.bfloat16, jnp.float32
     dma = pltpu.SemaphoreType.DMA
     final = pl.pallas_call(
-        functools.partial(block_kernel, n_rep, n_fsdp, n_tp),
+        functools.partial(block_kernel, n_rep, n_fsdp, n_tp, page),
         out_shape=jax.ShapeDtypeStruct((n_fsdp, local_rows, depth), f32),
         in_specs=[pl.BlockSpec(memory_space=pl.ANY)] * 8 + [pl.BlockSpec(memory_space=pltpu.VMEM)] * 7,
         out_specs=pl.BlockSpec(memory_space=pltpu.VMEM),
         scratch_shapes=[
             pltpu.VMEM((3, tiles, depth, TILE), bf16),
             pltpu.VMEM((SLOTS, 3, depth, TILE), f32),
+            pltpu.VMEM((2 * pages * page, kv_width), bf16),
+            pltpu.VMEM((local_rows, 2 * pages * page), f32),
             pltpu.VMEM((local_rows, width), f32),
             pltpu.VMEM((n_fsdp, 2 * local_rows, depth), f32),
             pltpu.VMEM((n_fsdp, 2 * local_rows, depth), f32),
@@ -623,9 +687,9 @@
         gain,
         start_rows,
         queries,
-        keys,
-        values,
-        valid,
+        kv,
+        page_table,
+        cache_len.reshape(local_rows, 1),
         fresh,
     )
     return final.transpose(1, 0, 2).reshape(local_rows, width).astype(jnp.bfloat16)

time: 143 us -> 128 us (0.90)
  local copies, waits for them, and re-layouts: 15.4 us -> 1.32 us
    slice x1 -> x0, local copies, waits for them, and re-layouts: 10.2 us -> none  [split_inputs(): values = kv_pool[:, :, 1, :].reshape(pages * page, kv_width)]
    unnamed x8 -> x0, local copies, waits for them, and re-layouts: 4.27 us -> none
    pallas_call x1, Pallas kernels: 125 us -> 124 us  [shards(): pl.pallas_call(functools.partial(block_kernel, n_rep, n_fsdp, n_tp, page)...]
where the time goes in v3:
time: 128 us
  Pallas kernels  124 us (97%)
  other arithmetic  3.03 us (2%)
  local copies, waits for them, and re-layouts  1.32 us (1%)
    pallas_call x1, Pallas kernels, shards(): pl.pallas_call(functools.partial(block_kernel, n_rep, n_fsdp, n_tp, page)...  124 us

profile of v3, /device:TPU:0, one launch (start us, length us, event | category | flops | bytes accessed | tf_op | source)
XLA Modules:
  0.0 128.0 jit_solution(9572978657704233030)
XLA Ops:
  0.0 1.3 %copy.17.length = s32[8,1]{1,0:T(8,128)} copy(s32[8,1]{0,1:T(1,128)} %bitcast.8) | data formatting | bytes 64 | tf_op jit(solution)/shard_map/reshape | solution.py:692
  1.3 1.5 %convert_bitcast_fusion.fresh = f32[2,2,8,1024]{3,2,1,0:T(8,128)} fusion(bf16[2,8,2,1024]{3,2,1,0:T(2,128)(2,1)} %param.26), kind=kLoop, calls=%fused_computation | loop fusion | flops 32768 | bytes 196608 | tf_op jit(solution)/shard_map/transpose | solution.py:613
  2.8 123.6 %update_and_decode.1 = f32[4,8,1024]{2,1,0:T(8,128)} custom-call(f32[2,1024,1792]{2,1,0:T(8,128)} %gu_master.1, f32[2,1024,1792]{2,1,0:T(8,128)} %gu_moment.1, f32[2,1024,1792]{2,1,0:T(8,128)} %gu_second.1, bf16[2,1024,1792]{2,1,0:T(8,128)(2,1)} %gu_grad.1, f32[1024,1792]{1,0:T(8,128)} %d_master.1, f32[1024,1792]{1,0:T(8,128)} %d_moment.1, ...), custom_call_target="tpu_custom_call" | custom-call | flops 5637144576 | bytes 77070336 | tf_op jit(solution)/shard_map/update_and_decode/pallas_call | solution.py:618
  126.4 1.5 %convert_element_type.10 = bf16[4,8,1024]{2,1,0:T(8,128)(2,1)} convert(f32[4,8,1024]{2,1,0:T(8,128)} %update_and_decode.1) | non-fusion elementwise | flops 32768 | bytes 196608 | tf_op jit(solution)/shard_map/convert_element_type | solution.py:695

commit v4 on v3

--- a/solution.py
+++ b/solution.py
@@ -21,7 +21,7 @@
 SUB = 32
 SQUARES = 128
 SLOTS = 4
-LAG = 3
+LAG = 4
 
 
 def block_kernel(
@@ -52,8 +52,6 @@
     att,
     pieces,
     got_pieces,
-    att_out,
-    att_in,
     sums,
     x,
     own,
@@ -73,8 +71,6 @@
     slot_sem,
     f_send,
     f_recv,
-    a_send,
-    a_recv,
     s_send,
     s_recv,
     x_send,
@@ -179,6 +175,21 @@
             src_ref=src, dst_ref=dst, send_sem=send, recv_sem=recv, device_id=dev, device_id_type=MESH
         )
 
+    def unpage(b, carry):
+        at = pl.ds(pl.multiple_of(b * 2 * page, 2 * page), 2 * page)
+        kv[at, :] = kv_raw[b].reshape(2 * page, kv.shape[1])
+        return carry
+
+    lax.fori_loop(0, kv_raw.shape[0], unpage, 0)
+
+    lane = lax.broadcasted_iota(jnp.int32, valid.shape, 1)
+    place = lax.rem(lane // 2, page)
+    held = jnp.zeros(valid.shape, jnp.float32)
+    for p in range(table.shape[1]):
+        named = table[:, p : p + 1] == lane // (2 * page)
+        held = jnp.where(named & (place + p * page < length[...]), 1.0, held)
+    valid[...] = jnp.where(lax.rem(lane, 2) == 0, held, 0.0)
+
     def squares_of(j, run):
         wait_all(grad_copies(j))
         for a in range(3):
@@ -211,43 +222,39 @@
             value = value + sums[base + k]
         return value
 
-    def unpage(b, carry):
-        at = pl.ds(pl.multiple_of(b * 2 * page, 2 * page), 2 * page)
-        kv[at, :] = kv_raw[b].reshape(2 * page, kv.shape[1])
-        return carry
-
-    lax.fori_loop(0, kv_raw.shape[0], unpage, 0)
-
-    lane = lax.broadcasted_iota(jnp.int32, valid.shape, 1)
-    place = lax.rem(lane // 2, page)
-    held = jnp.zeros(valid.shape, jnp.float32)
-    for p in range(table.shape[1]):
-        named = table[:, p : p + 1] == lane // (2 * page)
-        held = jnp.where(named & (place + p * page < length[...]), 1.0, held)
-    valid[...] = jnp.where(lax.rem(lane, 2) == 0, held, 0.0)
-
     heads = kv.shape[1] // HD
     group = width // kv.shape[1]
 
-    def attend(step, first, last):
+    def attend(first, last):
         scale = HD**-0.5
-        mask = jnp.concatenate([valid[...]] * group, axis=0) > 0.5
-        query = queries[step].astype(jnp.float32)
+        mask = jnp.concatenate([valid[...]] * (steps * group), axis=0) > 0.5
         for j in range(first, last):
             lanes = slice(j * HD, (j + 1) * HD)
-            q = jnp.concatenate(
-                [query[:, (j * group + i) * HD : (j * group + i + 1) * HD] for i in range(group)], axis=0
-            )
+            query = queries[:, :, j * group * HD : (j + 1) * group * HD].astype(jnp.float32)
+            q = [
+                jnp.concatenate([query[n, :, i * HD : (i + 1) * HD] for i in range(group)], axis=0)
+                for n in range(steps)
+            ]
             old = lax.dot_general(
-                q.astype(jnp.bfloat16), kv[:, lanes], (((1,), (1,)), ((), ())), preferred_element_type=jnp.float32
+                jnp.concatenate(q, axis=0).astype(jnp.bfloat16),
+                kv[:, lanes],
+                (((1,), (1,)), ((), ())),
+                preferred_element_type=jnp.float32,
             )
             old = jnp.where(mask, old * scale, -1e30)
+            new = []
+            for n in range(steps):
+                k = jnp.concatenate([fresh[n, 0, :, lanes]] * group, axis=0)
+                score = [
+                    jnp.sum(q[i] * k, axis=1, keepdims=True) * scale
+                    if n <= i
+                    else jnp.full((q[i].shape[0], 1), -1e30, jnp.float32)
+                    for i in range(steps)
+                ]
+                new.append(jnp.concatenate(score, axis=0))
             top = jnp.max(old, axis=1, keepdims=True)
-            new = []
-            for n in range(step + 1):
-                k = jnp.concatenate([fresh[n, 0, :, lanes]] * group, axis=0)
-                new.append(jnp.sum(q * k, axis=1, keepdims=True) * scale)
-                top = jnp.maximum(top, new[n])
+            for e in new:
+                top = jnp.maximum(top, e)
             old = jnp.exp(old - top)
             new = [jnp.exp(e - top) for e in new]
             whole = jnp.sum(old, axis=1, keepdims=True)
@@ -256,49 +263,50 @@
             inverse = 1.0 / whole
             prob = pltpu.roll(old * inverse, 1, 1).astype(jnp.bfloat16)
             y = jnp.dot(prob, kv[:, lanes], preferred_element_type=jnp.float32)
-            for n in range(step + 1):
-                v = jnp.concatenate([fresh[n, 1, :, lanes]] * group, axis=0)
+            for n in range(steps):
+                v = jnp.concatenate([fresh[n, 1, :, lanes]] * (group * steps), axis=0)
                 y = y + (new[n] * inverse).astype(jnp.bfloat16).astype(jnp.float32) * v
-            for i in range(group):
-                at = j * group + i
-                att[:, at * HD : (at + 1) * HD] = y[i * 8 : (i + 1) * 8, :]
+            for n in range(steps):
+                for i in range(group):
+                    at, row = j * group + i, (n * group + i) * 8
+                    att[n, :, at * HD : (at + 1) * HD] = y[row : row + 8, :]
 
     sum_copies = send_sums(tile_sum, 0, n_fsdp, f_dev)
-    attend(0, 0, heads)
+    attend(0, heads // 2)
     tile_sum = add_sums(sum_copies, tile_sum, 0, n_fsdp)
     sum_copies = send_sums(tile_sum, n_fsdp, n_group, g_dev)
-
-    blend = (start[...].astype(jnp.float32) + att[...]).astype(jnp.bfloat16).astype(jnp.float32)
+    attend(heads // 2, heads)
+
+    blend = (start[...].astype(jnp.float32) + att[0]).astype(jnp.bfloat16).astype(jnp.float32)
     factor = lax.rsqrt(jnp.sum(blend * blend, axis=1, keepdims=True) / width + norm_eps)
     for k in range(n_fsdp):
         cut = blend[:, k * depth : (k + 1) * depth]
         pieces[k, :8, :] = cut * factor * gain[k]
-        pieces[k, 8:, :] = cut
-    piece_copies = []
-    for k in range(1, n_fsdp):
-        there = lax.rem(f + k, n_fsdp)
-        piece_copies.append(
-            remote(pieces.at[there], got_pieces.at[k], f_send.at[k], f_recv.at[k], f_dev(k))
-        )
-    start_all(piece_copies)
+        pieces[k, 8:16, :] = cut
+        for n in range(1, steps):
+            pieces[k, (n + 1) * 8 : (n + 2) * 8, :] = att[n, :, k * depth : (k + 1) * depth]
+
+    def piece_copies():
+        return [
+            remote(
+                pieces.at[lax.rem(f + k, n_fsdp)], got_pieces.at[k], f_send.at[k], f_recv.at[k], f_dev(k)
+            )
+            for k in range(1, n_fsdp)
+        ]
+
+    start_all(piece_copies())
     got_pieces[0] = pieces[f]
-    wait_all(piece_copies)
 
     def joined(ref, a):
         at = pl.ds(a * 8, 8)
         blocks = [ref[lax.rem(f - b + n_fsdp, n_fsdp), at, :] for b in range(n_fsdp)]
         return jnp.concatenate(blocks, axis=0)
 
-    x[0, 0] = joined(got_pieces, 0).astype(jnp.bfloat16)
-    mixed[...] = joined(got_pieces, 1)
-
     def x_block(i):
         return x.at[i // x.shape[1], i % x.shape[1]]
 
-    def x_along_tp():
-        return [
-            remote(x_block(0), x_block(k), x_send.at[k], x_recv.at[k], z_dev(k)) for k in range(1, n_tp)
-        ]
+    def x_along_tp(k):
+        return remote(x_block(0), x_block(k), x_send.at[k], x_recv.at[k], z_dev(k))
 
     def x_along_rep(k):
         return [
@@ -307,19 +315,17 @@
         ]
 
     def x_start():
-        start_all(x_along_tp())
+        start_all([x_along_tp(k) for k in range(1, n_tp)])
         start_all(x_along_rep(0))
 
-    def x_forward():
-        for k, copy in enumerate(x_along_tp(), 1):
-            copy.wait()
-            start_all(x_along_rep(k))
+    def x_forward(k):
+        x_along_tp(k).wait()
+        start_all(x_along_rep(k))
 
     def x_finish():
         for k in range(n_tp):
             wait_all(x_along_rep(k))
 
-    x_start()
     tile_sum = add_sums(sum_copies, tile_sum, n_fsdp, n_group)
     clip = jnp.minimum(1.0, lax.rsqrt(jnp.sum(tile_sum, keepdims=True)))
 
@@ -442,9 +448,18 @@
             def _():
                 start_all(down_copies(2 * (j + SLOTS // 2 - tiles) + a))
 
-        @pl.when(j == LAG - 2)
+        @pl.when(j == 0)
         def _():
-            x_forward()
+            wait_all(piece_copies())
+            x[0, 0] = joined(got_pieces, 0).astype(jnp.bfloat16)
+            mixed[...] = joined(got_pieces, 1)
+            x_start()
+
+        for k in range(1, n_tp):
+
+            @pl.when(j == min(k, LAG))
+            def _(k=k):
+                x_forward(k)
 
         @pl.when(j == LAG)
         def _():
@@ -516,11 +531,7 @@
                 down_out[i] = own_block(i).astype(jnp.bfloat16)
             start_all(down_along_rep(k))
         summed = None
-        done = 0
-        for n, k in enumerate(order):
-            if step < steps - 1:
-                attend(step + 1, done, heads * (n + 1) // n_tp)
-                done = heads * (n + 1) // n_tp
+        for k in order:
             wait_all(down_along_rep(k))
             summed = own_block(k)
             for i in range(n_tp + k, n_group, n_tp):
@@ -528,25 +539,13 @@
             if k > 0:
                 down_out[k] = summed.astype(jnp.bfloat16)
                 down_along_tp(k).start()
-        if step < steps - 1:
-            for k in range(n_fsdp):
-                att_out[k] = att[:, k * depth : (k + 1) * depth]
-            att_copies = [
-                remote(
-                    att_out.at[lax.rem(f + k, n_fsdp)], att_in.at[k], a_send.at[k], a_recv.at[k], f_dev(k)
-                )
-                for k in range(1, n_fsdp)
-            ]
-            start_all(att_copies)
-            att_in[0] = att_out[f]
-            wait_all(att_copies)
         for k in range(1, n_tp):
             down_along_tp(k).wait()
             summed = summed + down_in[k].astype(jnp.float32)
         rows = (mixed[...] + summed).astype(jnp.bfloat16).astype(jnp.float32)
 
         if step < steps - 1:
-            blend = (rows + joined(att_in, 0)).astype(jnp.bfloat16).astype(jnp.float32)
+            blend = (rows + joined(got_pieces, 2 + step)).astype(jnp.bfloat16).astype(jnp.float32)
             mixed[...] = blend
             local = jnp.sum(blend * blend, axis=1, keepdims=True)
             squares[0] = jnp.broadcast_to(local, squares.shape[1:])
@@ -563,7 +562,8 @@
             factor = lax.rsqrt(whole[:, :1] / (depth * n_fsdp) + norm_eps)
             x[0, 0] = (mixed[...] * factor * gain[f]).astype(jnp.bfloat16)
             x_start()
-            x_forward()
+            for k in range(1, n_tp):
+                x_forward(k)
             x_finish()
         else:
             for k in range(n_fsdp):
@@ -625,11 +625,9 @@
             pltpu.VMEM((SLOTS, 3, depth, TILE), f32),
             pltpu.VMEM((2 * pages * page, kv_width), bf16),
             pltpu.VMEM((local_rows, 2 * pages * page), f32),
-            pltpu.VMEM((local_rows, width), f32),
-            pltpu.VMEM((n_fsdp, 2 * local_rows, depth), f32),
-            pltpu.VMEM((n_fsdp, 2 * local_rows, depth), f32),
-            pltpu.VMEM((n_fsdp, local_rows, depth), f32),
-            pltpu.VMEM((n_fsdp, local_rows, depth), f32),
+            pltpu.VMEM((steps, local_rows, width), f32),
+            pltpu.VMEM((n_fsdp, (steps + 1) * local_rows, depth), f32),
+            pltpu.VMEM((n_fsdp, (steps + 1) * local_rows, depth), f32),
             pltpu.VMEM((n_fsdp + n_group, 8, 128), f32),
             pltpu.VMEM((2, n_group // 2, block, depth), bf16),
             pltpu.VMEM((tiles, half, 2 * TILE), f32),
@@ -647,8 +645,6 @@
             pltpu.VMEM((n_fsdp, local_rows, depth), f32),
             dma((3, tiles)),
             dma((SLOTS, 3)),
-            dma((n_fsdp,)),
-            dma((n_fsdp,)),
             dma((n_fsdp,)),
             dma((n_fsdp,)),
             dma((n_fsdp + n_group,)),

time: 128 us -> 130 us (1.016)
    pallas_call x1, Pallas kernels: 124 us -> 125 us  [shards(): pl.pallas_call(functools.partial(block_kernel, n_rep, n_fsdp, n_tp, page)...]
where the time goes in v4:
time: 130 us; the launch traced here: 129 us
  Pallas kernels  125 us (96%)
  other arithmetic  3.03 us (2%)
  local copies, waits for them, and re-layouts  1.32 us (1%)
    pallas_call x1, Pallas kernels, shards(): pl.pallas_call(functools.partial(block_kernel, n_rep, n_fsdp, n_tp, page)...  125 us

profile of v4, /device:TPU:0, one launch (start us, length us, event | category | flops | bytes accessed | tf_op | source)
XLA Modules:
  0.0 129.3 jit_solution(18256705677149194604)
XLA Ops:
  0.0 1.3 %copy.17.length = s32[8,1]{1,0:T(8,128)} copy(s32[8,1]{0,1:T(1,128)} %bitcast.8) | data formatting | bytes 64 | tf_op jit(solution)/shard_map/reshape | solution.py:688
  1.3 1.5 %convert_bitcast_fusion.fresh = f32[2,2,8,1024]{3,2,1,0:T(8,128)} fusion(bf16[2,8,2,1024]{3,2,1,0:T(2,128)(2,1)} %param.26), kind=kLoop, calls=%fused_computation | loop fusion | flops 32768 | bytes 196608 | tf_op jit(solution)/shard_map/transpose | solution.py:613
  2.8 125.0 %update_and_decode.1 = f32[4,8,1024]{2,1,0:T(8,128)} custom-call(f32[2,1024,1792]{2,1,0:T(8,128)} %gu_master.1, f32[2,1024,1792]{2,1,0:T(8,128)} %gu_moment.1, f32[2,1024,1792]{2,1,0:T(8,128)} %gu_second.1, bf16[2,1024,1792]{2,1,0:T(8,128)(2,1)} %gu_grad.1, f32[1024,1792]{1,0:T(8,128)} %d_master.1, f32[1024,1792]{1,0:T(8,128)} %d_moment.1, ...), custom_call_target="tpu_custom_call" | custom-call | flops 5637144576 | bytes 77070336 | tf_op jit(solution)/shard_map/update_and_decode/pallas_call | solution.py:618
  127.8 1.5 %convert_element_type.10 = bf16[4,8,1024]{2,1,0:T(8,128)(2,1)} convert(f32[4,8,1024]{2,1,0:T(8,128)} %update_and_decode.1) | non-fusion elementwise | flops 32768 | bytes 196608 | tf_op jit(solution)/shard_map/convert_element_type | solution.py:691
